TPU v7x, 256 devices: a whole 4x4x8 slice. The times are simulated.
256 devices in a mesh: dp: 8 (over x, y_lo), tensor: 32 (over y_hi, z, core).
Axes of the slice: x: 4, y: 4 (y_hi: 2, y_lo: 2; y = y_hi * 2 + y_lo), z: 8, core: 2. Of those that a mesh axis runs over, the one named last changes fastest.
Arguments:
- tokens: bfloat16 [4096, 8192], P('dp', 'tensor'), may hold values from -6 to 6
- gate_in: bfloat16 [32, 256, 1024], P('tensor'), may hold values from -0.375 to 0.375
- gate_out: bfloat16 [32, 1024, 1024], P('tensor'), may hold values from -0.1875 to 0.1875
- up_in: bfloat16 [32, 256, 1024], P('tensor'), may hold values from -0.375 to 0.375
- up_out: bfloat16 [32, 1024, 1024], P('tensor'), may hold values from -0.1875 to 0.1875
- down_in: bfloat16 [32, 1024, 1024], P('tensor'), may hold values from -0.1875 to 0.1875
- down_out: bfloat16 [32, 1024, 256], P('tensor'), may hold values from -0.1875 to 0.1875
- cotangent: bfloat16 [4096, 8192], P('dp', 'tensor'), may hold values from -0.75 to 0.75
Outputs:
- output: bfloat16 [4096, 8192], P('dp', 'tensor')
- tokens_grad: bfloat16 [4096, 8192], P('dp', 'tensor')
- gate_in_grad: bfloat16 [32, 256, 1024], P('tensor', None, 'dp')
- gate_out_grad: bfloat16 [32, 1024, 1024], P('tensor', 'dp')
- up_in_grad: bfloat16 [32, 256, 1024], P('tensor', None, 'dp')
- up_out_grad: bfloat16 [32, 1024, 1024], P('tensor', 'dp')
- down_in_grad: bfloat16 [32, 1024, 1024], P('tensor', 'dp')
- down_out_grad: bfloat16 [32, 1024, 256], P('tensor', 'dp')
All inputs are finite; a program needn't handle non-finite values.
Results may differ from a plain program's by a relative error of at most 0.019.
Values may be sent and summed in bfloat16 or wider, within the bound.
A program may use at most 128 MiB of HBM per device.

v0:
```python
import jax
import jax.numpy as jnp
from jax import lax
from jax.sharding import PartitionSpec as P

NBLK = 32


def mult(form, left, right):
    return jnp.einsum(form, left, right, preferred_element_type=jnp.float32)


def rounded(value):
    return value.astype(jnp.bfloat16).astype(jnp.float32)


def per_device(tokens, gate_in, gate_out, up_in, up_out, down_in, down_out, cotangent):
    blocks = gate_in.shape[0]
    rows = tokens.shape[0]
    width = gate_in.shape[1]
    hidden_width = gate_in.shape[2]
    kwidth = hidden_width // NBLK
    xb = tokens.reshape(rows, blocks, width)
    rg = gate_in.reshape(blocks, width, NBLK, kwidth)
    ru = up_in.reshape(blocks, width, NBLK, kwidth)
    lg = gate_out.reshape(blocks, NBLK, kwidth, hidden_width)
    lu = up_out.reshape(blocks, NBLK, kwidth, hidden_width)
    rd = down_in.reshape(blocks, hidden_width, NBLK, kwidth)
    ld = down_out.reshape(blocks, NBLK, kwidth, width)
    gmid = mult("tbi,bick->cbkt", xb, rg).astype(jnp.bfloat16)
    umid = mult("tbi,bick->cbkt", xb, ru).astype(jnp.bfloat16)
    gmid, umid = (
        lax.all_to_all(gmid, "tensor", split_axis=0, concat_axis=1, tiled=True),
        lax.all_to_all(umid, "tensor", split_axis=0, concat_axis=1, tiled=True),
    )
    gate = mult("cbkt,cbkm->ctm", gmid, lg)
    upper = mult("cbkt,cbkm->ctm", umid, lu)
    sig = jax.nn.sigmoid(gate)
    act = gate * sig
    hidden = (act * upper).astype(jnp.bfloat16)
    dmid = mult("ctm,cmek->eckt", hidden, rd).astype(jnp.bfloat16)
    dmid = lax.all_to_all(dmid, "tensor", split_axis=0, concat_axis=1, tiled=True)
    output = mult("eckt,ecki->tei", dmid, ld).astype(jnp.bfloat16).reshape(rows, blocks * width)
    dyb = cotangent.reshape(rows, blocks, width)
    ddm = mult("tei,ecki->eckt", dyb, ld).astype(jnp.bfloat16)
    part_ld = rounded(mult("eckt,tei->ecki", dmid, dyb).reshape(blocks, hidden_width, width))
    ddm = lax.all_to_all(ddm, "tensor", split_axis=1, concat_axis=0, tiled=True)
    dhid = mult("eckt,cmek->ctm", ddm, rd)
    part_rd = rounded(
        mult("ctm,eckt->cmek", hidden, ddm).reshape(blocks, hidden_width, hidden_width)
    )
    dgate = (dhid * upper * sig * (1.0 + gate * (1.0 - sig))).astype(jnp.bfloat16)
    dup = (dhid * act).astype(jnp.bfloat16)
    part_lg = rounded(
        mult("cbkt,ctm->cbkm", gmid, dgate).reshape(blocks, hidden_width, hidden_width)
    )
    part_lu = rounded(mult("cbkt,ctm->cbkm", umid, dup).reshape(blocks, hidden_width, hidden_width))
    dgm = mult("cbkm,ctm->cbkt", lg, dgate).astype(jnp.bfloat16)
    dum = mult("cbkm,ctm->cbkt", lu, dup).astype(jnp.bfloat16)
    dgm, dum = (
        lax.all_to_all(dgm, "tensor", split_axis=1, concat_axis=0, tiled=True),
        lax.all_to_all(dum, "tensor", split_axis=1, concat_axis=0, tiled=True),
    )
    part_rg = rounded(mult("tbi,cbkt->bick", xb, dgm).reshape(blocks, width, hidden_width))
    part_ru = rounded(mult("tbi,cbkt->bick", xb, dum).reshape(blocks, width, hidden_width))
    dx = mult("cbkt,bick->tbi", dgm, rg) + mult("cbkt,bick->tbi", dum, ru)
    tokens_grad = dx.astype(jnp.bfloat16).reshape(rows, blocks * width)
    sum_rg, sum_lg, sum_ru, sum_lu, sum_rd, sum_ld = (
        lax.psum_scatter(
            part_rg.astype(jnp.bfloat16), "dp", scatter_dimension=2, tiled=True
        ).astype(jnp.float32),
        lax.psum_scatter(
            part_lg.astype(jnp.bfloat16), "dp", scatter_dimension=1, tiled=True
        ).astype(jnp.float32),
        lax.psum_scatter(
            part_ru.astype(jnp.bfloat16), "dp", scatter_dimension=2, tiled=True
        ).astype(jnp.float32),
        lax.psum_scatter(
            part_lu.astype(jnp.bfloat16), "dp", scatter_dimension=1, tiled=True
        ).astype(jnp.float32),
        lax.psum_scatter(
            part_rd.astype(jnp.bfloat16), "dp", scatter_dimension=1, tiled=True
        ).astype(jnp.float32),
        lax.psum_scatter(
            part_ld.astype(jnp.bfloat16), "dp", scatter_dimension=1, tiled=True
        ).astype(jnp.float32),
    )
    return (
        output,
        tokens_grad,
        sum_rg.astype(jnp.bfloat16),
        sum_lg.astype(jnp.bfloat16),
        sum_ru.astype(jnp.bfloat16),
        sum_lu.astype(jnp.bfloat16),
        sum_rd.astype(jnp.bfloat16),
        sum_ld.astype(jnp.bfloat16),
    )


def solution(mesh):
    in_specs = (
        P("dp", "tensor"),
        P("tensor", None, None),
        P("tensor", None, None),
        P("tensor", None, None),
        P("tensor", None, None),
        P("tensor", None, None),
        P("tensor", None, None),
        P("dp", "tensor"),
    )
    out_specs = (
        P("dp", "tensor"),
        P("dp", "tensor"),
        P("tensor", None, "dp"),
        P("tensor", "dp", None),
        P("tensor", None, "dp"),
        P("tensor", "dp", None),
        P("tensor", "dp", None),
        P("tensor", "dp", None),
    )
    return jax.shard_map(
        per_device, mesh=mesh, in_specs=in_specs, out_specs=out_specs, check_vma=False
    )
```

profile of v0, /device:TPU:1, one launch (start us, length us, event | category | flops | bytes accessed | tf_op | source)
XLA Modules:
  0.0 512.3 jit_solution(7754907620138736127)
XLA Ops:
  7.2 0.0 copy-start
  7.2 1.4 copy.31
  8.6 0.0 copy-start.2
  8.6 0.0 copy-start.1
  8.6 2.6 fusion.14
  11.2 0.0 copy-done.2
  11.2 12.8 %all-to-all-start.1 = ((bf16[32,1,32,512]{3,2,1,0:T(8,128)(2,1)}), bf16[32,1,32,512]{3,2,1,0:T(8,128)(2,1)S(1)}, u32[]{:S(2)}, u32[]{:S(2)}) async-start(bf16[32,1,32,512]{3,2,1,0:T(8,128)(2,1)} %fusion.14), calls=%async_computation.1 | async-start | bytes 2097152 | tf_op jit(solution)/shard_map/all_to_all | solution.py:34
  24.0 2.1 copy.29
  26.0 0.0 copy-done.1
  26.0 2.5 fusion.13
  28.5 23.2 %all-to-all-done.1 = bf16[32,1,32,512]{3,2,1,0:T(8,128)(2,1)S(1)} async-done(((bf16[32,1,32,512]{3,2,1,0:T(8,128)(2,1)}), bf16[32,1,32,512]{3,2,1,0:T(8,128)(2,1)S(1)}, u32[]{:S(2)}, u32[]{:S(2)}) %all-to-all-start.1) | async-done | bytes 1048608 | tf_op jit(solution)/shard_map/all_to_all | solution.py:34
  51.7 6.6 %all-to-all-start = ((bf16[32,1,32,512]{3,2,1,0:T(8,128)(2,1)}), bf16[32,1,32,512]{3,2,1,0:T(8,128)(2,1)}, u32[]{:S(2)}, u32[]{:S(2)}) async-start(bf16[32,1,32,512]{3,2,1,0:T(8,128)(2,1)} %fusion.13), calls=%async_computation | async-start | bytes 2097152 | tf_op jit(solution)/shard_map/all_to_all | solution.py:33
  58.3 2.6 fusion.15
  60.9 25.4 %all-to-all-done = bf16[32,1,32,512]{3,2,1,0:T(8,128)(2,1)} async-done(((bf16[32,1,32,512]{3,2,1,0:T(8,128)(2,1)}), bf16[32,1,32,512]{3,2,1,0:T(8,128)(2,1)}, u32[]{:S(2)}, u32[]{:S(2)}) %all-to-all-start) | async-done | bytes 1048608 | tf_op jit(solution)/shard_map/all_to_all | solution.py:33
  86.3 6.6 %all-to-all-start.3 = ((bf16[1,32,32,512]{3,2,0,1:T(8,128)(2,1)}), bf16[1,32,32,512]{3,2,0,1:T(8,128)(2,1)}, u32[]{:S(2)}, u32[]{:S(2)}) async-start(bf16[1,32,32,512]{3,2,0,1:T(8,128)(2,1)} %fusion.15), calls=%async_computation.3 | async-start | bytes 2097152 | tf_op jit(solution)/shard_map/all_to_all | solution.py:47
  92.8 4.0 copy.33
  96.8 0.0 copy-done
  96.8 4.0 fusion.31
  100.8 0.0 copy-done.5
  100.8 2.6 fusion.29
  103.5 17.3 %all-to-all-done.3 = bf16[1,32,32,512]{3,2,0,1:T(8,128)(2,1)} async-done(((bf16[1,32,32,512]{3,2,0,1:T(8,128)(2,1)}), bf16[1,32,32,512]{3,2,0,1:T(8,128)(2,1)}, u32[]{:S(2)}, u32[]{:S(2)}) %all-to-all-start.3) | async-done | bytes 1048608 | tf_op jit(solution)/shard_map/all_to_all | solution.py:47
  120.8 6.5 %fusion.4 = (bf16[512,1024]{1,0:T(8,128)(2,1)S(1)}, bf16[512,1024]{1,0:T(8,128)(2,1)}, bf16[512,1024]{1,0:T(8,128)(2,1)}) fusion(f32[512,1024,1]{1,0,2:T(8,128)} %fusion.29, f32[512,1024,1]{1,0,2:T(8,128)} %fusion.31, bf16[1024,32,32]{0,2,1:T(8,128)(2,1)} %bitcast.182, bf16[1,32,32,512]{3,2,0,1:T(8,128)(2,1)} %all-to-all-done.3), kind=kOutput, calls=%fused_computation.6 | convolution fusion | flops 1081606144 | bytes 10485760 | tf_op jit(solution)/shard_map/eckt,cmek->ctm/dot_general | solution.py:10
  127.3 1.0 copy-done.7
  128.3 2.3 fusion.11
  130.5 6.6 %all-to-all-start.4 = ((bf16[1,32,32,512]{3,2,0,1:T(8,128)(2,1)}), bf16[1,32,32,512]{3,2,0,1:T(8,128)(2,1)}, u32[]{:S(2)}, u32[]{:S(2)}) async-start(bf16[1,32,32,512]{3,2,0,1:T(8,128)(2,1)} %fusion.11), calls=%async_computation.4 | async-start | bytes 2097152 | tf_op jit(solution)/shard_map/all_to_all | solution.py:61
  137.1 4.3 fusion.12
  141.4 23.7 %all-to-all-done.4 = bf16[1,32,32,512]{3,2,0,1:T(8,128)(2,1)} async-done(((bf16[1,32,32,512]{3,2,0,1:T(8,128)(2,1)}), bf16[1,32,32,512]{3,2,0,1:T(8,128)(2,1)}, u32[]{:S(2)}, u32[]{:S(2)}) %all-to-all-start.4) | async-done | bytes 1048608 | tf_op jit(solution)/shard_map/all_to_all | solution.py:61
  165.1 6.6 %all-to-all-start.5 = ((bf16[1,32,32,512]{3,2,0,1:T(8,128)(2,1)}), bf16[1,32,32,512]{3,2,0,1:T(8,128)(2,1)}, u32[]{:S(2)}, u32[]{:S(2)}) async-start(bf16[1,32,32,512]{3,2,0,1:T(8,128)(2,1)} %fusion.12), calls=%async_computation.5 | async-start | bytes 2097152 | tf_op jit(solution)/shard_map/all_to_all | solution.py:62
  171.6 3.2 fusion
  174.9 1.2 convert_bitcast_fusion.3
  176.1 23.5 %all-to-all-done.5 = bf16[1,32,32,512]{3,2,0,1:T(8,128)(2,1)} async-done(((bf16[1,32,32,512]{3,2,0,1:T(8,128)(2,1)}), bf16[1,32,32,512]{3,2,0,1:T(8,128)(2,1)}, u32[]{:S(2)}, u32[]{:S(2)}) %all-to-all-start.5) | async-done | bytes 1048608 | tf_op jit(solution)/shard_map/all_to_all | solution.py:62
  199.6 6.8 %all-to-all-start.2 = ((bf16[32,1,32,512]{3,2,1,0:T(8,128)(2,1)}), bf16[32,1,32,512]{3,2,1,0:T(8,128)(2,1)}, u32[]{:S(2)}, u32[]{:S(2)}) async-start(bf16[32,1,32,512]{3,2,1,0:T(8,128)(2,1)} %convert_bitcast_fusion.3), calls=%async_computation.2 | async-start | bytes 2097152 | tf_op jit(solution)/shard_map/all_to_all | solution.py:42
  206.3 0.0 reduce-scatter.7.cloned.1.call-start
  206.4 2.5 fusion.16
  208.8 0.0 reduce-scatter.7.cloned.1.call-update
  208.9 0.0 reduce-scatter.11.cloned.1.call-start
  208.9 2.5 fusion.17
  211.4 0.0 reduce-scatter.11.cloned.1.call-update
  211.5 0.0 reduce-scatter.17.cloned.1.call-start
  211.5 22.8 %all-to-all-done.2 = bf16[32,1,32,512]{3,2,1,0:T(8,128)(2,1)} async-done(((bf16[32,1,32,512]{3,2,1,0:T(8,128)(2,1)}), bf16[32,1,32,512]{3,2,1,0:T(8,128)(2,1)}, u32[]{:S(2)}, u32[]{:S(2)}) %all-to-all-start.2) | async-done | bytes 1048608 | tf_op jit(solution)/shard_map/all_to_all | solution.py:42
  234.3 2.5 fusion.18
  236.8 0.0 reduce-scatter.17.cloned.1.call-update
  236.8 0.0 reduce-scatter.9.cloned.1.call-start
  236.9 4.2 convert_bitcast_fusion.2
  241.1 0.0 reduce-scatter.9.cloned.1.call-update
  241.1 0.0 reduce-scatter.15.cloned.1.call-start
  241.1 4.3 convert_bitcast_fusion
  245.4 0.0 reduce-scatter.15.cloned.1.call-update
  245.4 0.0 reduce-scatter.13.cloned.1.call-start
  245.5 3.8 convert_bitcast_fusion.1
  249.2 0.0 reduce-scatter.13.cloned.1.call-update
  249.3 1.0 copy-done.6
  250.3 2.5 fusion.21
  252.8 0.0 copy-done.3
  252.8 1.8 convolution_bitcast_fusion
  254.5 0.0 copy-done.4
  254.5 2.4 fusion.20
  256.9 1.6 copy.38
  258.5 29.5 %reduce-scatter.11.cloned.1.call-done = bf16[1,256,128]{1,2,0:T(8,128)(2,1)} async-done(((bf16[1,256,1024]{1,2,0:T(8,128)(2,1)}), bf16[1,256,128]{1,2,0:T(8,128)(2,1)}) %reduce-scatter.11.cloned.1.call-update) | async-done | bytes 65552 | tf_op jit(solution)/shard_map/reduce_scatter | solution.py:75
  288.1 1.6 copy.39
  289.6 40.5 %reduce-scatter.17.cloned.1.call-done = bf16[1,128,256]{2,1,0:T(8,128)(2,1)} async-done(((bf16[1,1024,256]{2,1,0:T(8,128)(2,1)}), bf16[1,128,256]{2,1,0:T(8,128)(2,1)}) %reduce-scatter.17.cloned.1.call-update) | async-done | bytes 65552 | tf_op jit(solution)/shard_map/reduce_scatter | solution.py:84
  330.1 59.6 %reduce-scatter.9.cloned.1.call-done = bf16[1,128,1024]{2,1,0:T(8,128)(2,1)} async-done(((bf16[1,1024,1024]{2,1,0:T(8,128)(2,1)}), bf16[1,128,1024]{2,1,0:T(8,128)(2,1)}) %reduce-scatter.9.cloned.1.call-update) | async-done | bytes 262160 | tf_op jit(solution)/shard_map/reduce_scatter | solution.py:72
  389.8 58.1 %reduce-scatter.15.cloned.1.call-done = bf16[1,128,1024]{2,1,0:T(8,128)(2,1)} async-done(((bf16[1,1024,1024]{2,1,0:T(8,128)(2,1)}), bf16[1,128,1024]{2,1,0:T(8,128)(2,1)}) %reduce-scatter.15.cloned.1.call-update) | async-done | bytes 262160 | tf_op jit(solution)/shard_map/reduce_scatter | solution.py:81
  447.8 57.6 %reduce-scatter.13.cloned.1.call-done = bf16[1,128,1024]{2,1,0:T(8,128)(2,1)} async-done(((bf16[1,1024,1024]{2,1,0:T(8,128)(2,1)}), bf16[1,128,1024]{2,1,0:T(8,128)(2,1)}) %reduce-scatter.13.cloned.1.call-update) | async-done | bytes 262160 | tf_op jit(solution)/shard_map/reduce_scatter | solution.py:78
  (6 shorter events, 0.0 us)
Async XLA Ops:
  7.2 89.6 %copy-start = (bf16[1,1024,1024]{2,1,0:T(8,128)(2,1)S(1)}, bf16[1,1024,1024]{2,1,0:T(8,128)(2,1)}, u32[]{:S(2)}) copy-start(bf16[1,1024,1024]{2,1,0:T(8,128)(2,1)} %param.10) | copy-start | bytes 6291460
  8.6 2.6 copy-start.2
  8.6 17.4 %copy-start.1 = (bf16[512,256]{1,0:T(8,128)(2,1)S(1)}, bf16[512,256]{1,0:T(8,128)(2,1)}, u32[]{:S(2)}) copy-start(bf16[512,256]{1,0:T(8,128)(2,1)} %param.8) | copy-start | bytes 786436
  11.2 40.5 %all-to-all-start.1 = ((bf16[32,1,32,512]{3,2,1,0:T(8,128)(2,1)}), bf16[32,1,32,512]{3,2,1,0:T(8,128)(2,1)S(1)}, u32[]{:S(2)}, u32[]{:S(2)}) async-start(bf16[32,1,32,512]{3,2,1,0:T(8,128)(2,1)} %fusion.14), calls=%async_computation.1 | async-start | bytes 2097152 | tf_op jit(solution)/shard_map/all_to_all | solution.py:34
  51.7 34.6 %all-to-all-start = ((bf16[32,1,32,512]{3,2,1,0:T(8,128)(2,1)}), bf16[32,1,32,512]{3,2,1,0:T(8,128)(2,1)}, u32[]{:S(2)}, u32[]{:S(2)}) async-start(bf16[32,1,32,512]{3,2,1,0:T(8,128)(2,1)} %fusion.13), calls=%async_computation | async-start | bytes 2097152 | tf_op jit(solution)/shard_map/all_to_all | solution.py:33
  86.3 34.5 %all-to-all-start.3 = ((bf16[1,32,32,512]{3,2,0,1:T(8,128)(2,1)}), bf16[1,32,32,512]{3,2,0,1:T(8,128)(2,1)}, u32[]{:S(2)}, u32[]{:S(2)}) async-start(bf16[1,32,32,512]{3,2,0,1:T(8,128)(2,1)} %fusion.15), calls=%async_computation.3 | async-start | bytes 2097152 | tf_op jit(solution)/shard_map/all_to_all | solution.py:47
  96.8 4.0 copy-start.5
  127.3 1.0 copy-start.7
  130.5 34.5 %all-to-all-start.4 = ((bf16[1,32,32,512]{3,2,0,1:T(8,128)(2,1)}), bf16[1,32,32,512]{3,2,0,1:T(8,128)(2,1)}, u32[]{:S(2)}, u32[]{:S(2)}) async-start(bf16[1,32,32,512]{3,2,0,1:T(8,128)(2,1)} %fusion.11), calls=%async_computation.4 | async-start | bytes 2097152 | tf_op jit(solution)/shard_map/all_to_all | solution.py:61
  165.1 34.5 %all-to-all-start.5 = ((bf16[1,32,32,512]{3,2,0,1:T(8,128)(2,1)}), bf16[1,32,32,512]{3,2,0,1:T(8,128)(2,1)}, u32[]{:S(2)}, u32[]{:S(2)}) async-start(bf16[1,32,32,512]{3,2,0,1:T(8,128)(2,1)} %fusion.12), calls=%async_computation.5 | async-start | bytes 2097152 | tf_op jit(solution)/shard_map/all_to_all | solution.py:62
  199.6 34.7 %all-to-all-start.2 = ((bf16[32,1,32,512]{3,2,1,0:T(8,128)(2,1)}), bf16[32,1,32,512]{3,2,1,0:T(8,128)(2,1)}, u32[]{:S(2)}, u32[]{:S(2)}) async-start(bf16[32,1,32,512]{3,2,1,0:T(8,128)(2,1)} %convert_bitcast_fusion.3), calls=%async_computation.2 | async-start | bytes 2097152 | tf_op jit(solution)/shard_map/all_to_all | solution.py:42
  206.3 50.6 %reduce-scatter.7.cloned.1.call-start = ((), (), s32[]{:S(2)}) async-start(), calls=%async_computation.12 | async-start | bytes 589824 | tf_op jit(solution)/shard_map/reduce_scatter | solution.py:69
  208.9 79.2 %reduce-scatter.11.cloned.1.call-start = ((), (), s32[]{:S(2)}) async-start(), calls=%async_computation.14 | async-start | bytes 589824 | tf_op jit(solution)/shard_map/reduce_scatter | solution.py:75
  211.5 118.7 %reduce-scatter.17.cloned.1.call-start = ((), (), s32[]{:S(2)}) async-start(), calls=%async_computation.17 | async-start | bytes 589824 | tf_op jit(solution)/shard_map/reduce_scatter | solution.py:84
  236.8 152.9 %reduce-scatter.9.cloned.1.call-start = ((), (), s32[]{:S(2)}) async-start(), calls=%async_computation.13 | async-start | bytes 2359296 | tf_op jit(solution)/shard_map/reduce_scatter | solution.py:72
  241.1 206.8 %reduce-scatter.15.cloned.1.call-start = ((), (), s32[]{:S(2)}) async-start(), calls=%async_computation.16 | async-start | bytes 2359296 | tf_op jit(solution)/shard_map/reduce_scatter | solution.py:81
  245.4 260.1 %reduce-scatter.13.cloned.1.call-start = ((), (), s32[]{:S(2)}) async-start(), calls=%async_computation.15 | async-start | bytes 2359296 | tf_op jit(solution)/shard_map/reduce_scatter | solution.py:78
  249.2 1.0 copy-start.6
  250.3 2.5 copy-start.3
  252.8 1.8 copy-start.4
Sparse Core Ops, SparseCore 0:
  209.7 37.6 reduce-scatter.6
  250.0 37.9 reduce-scatter.10
  291.2 38.9 reduce-scatter.16
  333.3 56.4 reduce-scatter.8
  392.9 54.9 reduce-scatter.14
  451.0 54.4 reduce-scatter.12
where the time goes:
time: 514 us; the launch traced here: 512 us
  waiting for transfers between devices  381 us (74%)
  matrix products  56.9 us (11%)
  starting transfers between devices  46.1 us (9%)
  between operations  14.2 us (3%)
  local copies, waits for them, and re-layouts  12.6 us (2%)
    reduce_scatter x1, waiting for transfers between devices, per_device(): lax.psum_scatter(part_lg.astype(jnp.bfloat16), 'dp', scatter_dimension=1,...  59.6 us
    reduce_scatter x1, waiting for transfers between devices, per_device(): lax.psum_scatter(part_rd.astype(jnp.bfloat16), 'dp', scatter_dimension=1,...  58.1 us
    reduce_scatter x1, waiting for transfers between devices, per_device(): lax.psum_scatter(part_lu.astype(jnp.bfloat16), 'dp', scatter_dimension=1,...  57.6 us
    dot_general x17, matrix products, mult(): return jnp.einsum(form, left, right, preferred_element_type=jnp.float32)  53.7 us
    reduce_scatter x1, waiting for transfers between devices, per_device(): lax.psum_scatter(part_ld.astype(jnp.bfloat16), 'dp', scatter_dimension=1,...  40.5 us
    reduce_scatter x1, waiting for transfers between devices, per_device(): lax.psum_scatter(part_ru.astype(jnp.bfloat16), 'dp', scatter_dimension=2,...  29.5 us
    all_to_all x1, waiting for transfers between devices, per_device(): lax.all_to_all(gmid, 'tensor', split_axis=0, concat_axis=1, tiled=True)  25.4 us
    all_to_all x1, waiting for transfers between devices, per_device(): lax.all_to_all(dgm, 'tensor', split_axis=1, concat_axis=0, tiled=True)  23.7 us
  transfers between devices with their start and end apart: 12, of which 11 were waited for; matrix products, arithmetic and copies ran while one was open for 11% of the time, Pallas kernels for 0%

commit v1 on v0

v1 whole, which is shorter than its diff:
```python
import jax
import jax.numpy as jnp
from jax import lax
from jax.experimental import pallas as pl
from jax.experimental.pallas import tpu as pltpu
from jax.sharding import PartitionSpec as P

MESH = pl.DeviceIdType.MESH
BF = jnp.bfloat16
F32 = jnp.float32
NT = (((1,), (1,)), ((), ()))
NN = (((1,), (0,)), ((), ()))
TOK, DB, MB, KW, NBLK, NDP = 512, 256, 1024, 32, 32, 8


def dot(a, b, form=NN):
    return lax.dot_general(a, b, form, preferred_element_type=F32)


def rows_at(index, size):
    return pl.ds(pl.multiple_of(index * size, size), size)


def tiles(count, body):
    def step(i, carry):
        body(i)
        return carry

    lax.fori_loop(0, count, step, 0)


def kernel(
    x_h, rg_h, lg_h, ru_h, lu_h, rd_h, ld_h, dy_h,
    out_o, dx_o, rg_o, lg_o, ru_o, lu_o, rd_o, ld_o,
    x, rg, lg, ru, lu, rd, ld, dy,
    xt, lgt, lut, rdt, ldt,
    send, recv,
    gate, upper, hidden, dgate, dup, dxt,
    p2, pn, pp, ysend, ra, rb, rc, rdn, ye,
    small, rsmall,
    load_sem, a2a_send, a2a_recv, ring_send, ring_recv, small_send, small_recv,
):
    dp, tn = lax.axis_index("dp"), lax.axis_index("tensor")
    xc, yl = dp // 2, dp % 2
    yh, z, core = tn // 16, (tn // 2) % 8, tn % 2

    loads = {}
    for i, (name, src, dst) in enumerate((
        ("x", x_h, x), ("rg", rg_h.at[0], rg), ("ru", ru_h.at[0], ru), ("dy", dy_h, dy), ("ld", ld_h.at[0], ld),
        ("lg", lg_h.at[0], lg), ("lu", lu_h.at[0], lu), ("rd", rd_h.at[0], rd),
    )):
        loads[name] = pltpu.make_async_copy(src, dst, load_sem.at[i])
        loads[name].start()

    def peer(j):
        g = j // 4
        dz = 4 + (1 - 2 * (g % 2)) * ((g + 1) // 2)
        py = (yh + 1 - (j // 2) % 2) % 2
        pz = (z + dz) % 8
        pc = (core + 1 - j % 2) % 2
        return (py * 8 + pz) * 2 + pc

    def dp_peer(j):
        return (dp + 1 + j) % NDP

    barrier = pltpu.get_barrier_semaphore()

    def greet_tensor(j):
        pl.semaphore_signal(barrier, inc=1, device_id=(dp, peer(j)), device_id_type=MESH)

    def greet_dp(j):
        pl.semaphore_signal(barrier, inc=1, device_id=(dp_peer(j), tn), device_id_type=MESH)

    tiles(NBLK - 1, greet_tensor)
    tiles(NDP - 1, greet_dp)

    def exchange(i):
        mine = rows_at(tn, KW)

        def one(j):
            to = peer(j)
            pltpu.make_async_remote_copy(
                src_ref=send.at[i, rows_at(to, KW)], dst_ref=recv.at[i, mine],
                send_sem=a2a_send.at[i], recv_sem=a2a_recv.at[i],
                device_id=(dp, to), device_id_type=MESH,
            ).start()

        tiles(NBLK - 1, one)
        recv[i, mine, :] = send[i, mine, :]

    def await_bytes(ref, sem):
        pltpu.make_async_copy(ref, ref, sem).wait()

    def arrived(i):
        await_bytes(recv.at[i, pl.ds(0, MB - KW)], a2a_recv.at[i])

    GM, UM, DD, DM, DG, DU = range(6)

    def first(i, w):
        def body(q):
            cols = rows_at(q, 256)
            send[i, cols, :] = dot(w[:, cols].T, x[...], NT).astype(BF)

        tiles(4, body)

    loads["x"].wait()
    loads["rg"].wait()
    first(GM, rg)
    pl.semaphore_wait(barrier, NBLK - 1 + NDP - 1)
    exchange(GM)
    loads["ru"].wait()
    first(UM, ru)
    exchange(UM)
    loads["dy"].wait()
    loads["ld"].wait()

    def back_down(q):
        rows = rows_at(q, 256)
        send[DD, rows, :] = dot(ld[rows, :], dy[...], NT).astype(BF)

    tiles(4, back_down)
    exchange(DD)

    def flip(src, dst, across, down):
        def body(i):
            r, c = i // across, i % across
            dst[rows_at(c, 256), rows_at(r, 256)] = src[rows_at(r, 256), rows_at(c, 256)].T

        tiles(across * down, body)

    loads["lg"].wait()
    flip(lg, lgt, 4, 4)
    loads["lu"].wait()
    flip(lu, lut, 4, 4)
    loads["rd"].wait()
    flip(rd, rdt, 4, 4)
    flip(x, xt, 1, 2)
    flip(ld, ldt, 1, 4)

    arrived(GM)
    arrived(UM)

    def forward(q):
        rows = rows_at(q, 256)
        g = dot(lgt[rows, :], recv[GM])
        u = dot(lut[rows, :], recv[UM])
        gate[rows, :] = g
        upper[rows, :] = u
        hidden[rows, :] = (g * jax.nn.sigmoid(g) * u).astype(BF)

    tiles(4, forward)

    def down(q):
        rows = rows_at(q, 256)
        send[DM, rows, :] = dot(rdt[rows, :], hidden[...]).astype(BF)

    tiles(4, down)
    exchange(DM)

    arrived(DD)

    def backward(q):
        rows = rows_at(q, 256)
        dh = dot(rd[rows, :], recv[DD])
        g, u = gate[rows, :], upper[rows, :]
        s = jax.nn.sigmoid(g)
        dgate[rows, :] = (dh * u * s * (1.0 + g * (1.0 - s))).astype(BF)
        dup[rows, :] = (dh * (g * s)).astype(BF)

    tiles(4, backward)

    def mids(i, w, d):
        def body(q):
            rows = rows_at(q, 256)
            send[i, rows, :] = dot(w[rows, :], d[...]).astype(BF)

        tiles(4, body)
        exchange(i)

    mids(DG, lg, dgate)
    mids(DU, lu, dup)

    nxt, prv, opp = (xc + 1) % 4, (xc + 3) % 4, (xc + 2) % 4

    def ship(src, dst, sem, to):
        cp = pltpu.make_async_remote_copy(
            src_ref=src, dst_ref=dst, send_sem=ring_send.at[sem], recv_sem=ring_recv.at[sem],
            device_id=to, device_id_type=MESH,
        )
        cp.start()
        return cp

    to_next, to_prev = (nxt * 2 + yl, tn), (prv * 2 + yl, tn)
    to_pair = (xc * 2 + 1 - yl, tn)
    big = (
        (hidden, recv.at[DD], rd_o),
        (recv.at[GM], dgate, lg_o),
        (recv.at[UM], dup, lu_o),
    )
    ships = []

    def quarter(a, left, right, q, put):
        def body(h):
            rows = pl.ds(pl.multiple_of(q * 256 + h * 128, 128), 128)
            put(h, dot(left[rows, :], right[...], NT))

        tiles(2, body)

    started = [[None] * 5 for _ in big]
    for a, (left, right, _) in enumerate(big):
        def put(h, v, a=a):
            p2[a, h] = v.astype(BF)

        quarter(a, left, right, opp, put)
        started[a][0] = ship(p2.at[a, 0], ra.at[a], 5 * a, to_next)
        started[a][1] = ship(p2.at[a, 1], rb.at[a], 5 * a + 1, to_prev)
    for a, (left, right, _) in enumerate(big):
        def put_n(h, v, a=a):
            pn[a, h] = v.astype(BF)

        def put_p(h, v, a=a):
            pp[a, h] = v.astype(BF)

        quarter(a, left, right, nxt, put_n)
        started[a][0].wait_recv()
        pn[a, 0] = (pn[a, 0].astype(F32) + ra[a].astype(F32)).astype(BF)
        started[a][2] = ship(pn.at[a], rc.at[a], 5 * a + 2, to_next)
        quarter(a, left, right, prv, put_p)
        started[a][1].wait_recv()
        pp[a, 1] = (pp[a, 1].astype(F32) + rb[a].astype(F32)).astype(BF)
        started[a][3] = ship(pp.at[a], rdn.at[a], 5 * a + 3, to_prev)
    for a, (left, right, out) in enumerate(big):
        started[a][2].wait_recv()
        started[a][3].wait_recv()

        def total(h, a=a, left=left, right=right):
            rows = pl.ds(pl.multiple_of(xc * 256 + h * 128, 128), 128)
            return dot(left[rows, :], right[...], NT) + rc[a, h].astype(F32) + rdn[a, h].astype(F32)

        ysend[a] = total(1 - yl).astype(BF)
        started[a][4] = ship(ysend.at[a], ye.at[a], 5 * a + 4, to_pair)
        own = total(yl)
        upper[pl.ds(a * 256, 128), :] = own[:, 0:TOK]
        upper[pl.ds(a * 256 + 128, 128), :] = own[:, TOK:]

    def scatter(s):
        def one(j):
            to = dp_peer(j)
            pltpu.make_async_remote_copy(
                src_ref=small.at[s, to], dst_ref=rsmall.at[s, dp],
                send_sem=small_send.at[s], recv_sem=small_recv.at[s],
                device_id=(to, tn), device_id_type=MESH,
            ).start()

        tiles(NDP - 1, one)
        rsmall[s, dp] = small[s, dp]

    arrived(DM)

    def part_ld(d):
        v = dot(recv[DM, rows_at(d, 128), :], dy[...]).astype(BF)
        small[0, d, :, :] = v

    tiles(NDP, part_ld)
    scatter(0)
    out_o[...] = dot(ldt[...], recv[DM]).T.astype(BF)

    def part_in(s, i):
        def body(q):
            v = dot(xt[...], recv[i, rows_at(q, 256), :], NT).astype(BF)
            small[s, 2 * q, :, :] = jnp.concatenate([v[0:128, 0:128], v[128:256, 0:128]], axis=1)
            small[s, 2 * q + 1, :, :] = jnp.concatenate([v[0:128, 128:256], v[128:256, 128:256]], axis=1)

        tiles(4, body)
        scatter(s)

    arrived(DG)
    part_in(1, DG)
    dxt[...] = dot(rg[...], recv[DG])
    arrived(DU)
    part_in(2, DU)
    dx_o[...] = (dxt[...] + dot(ru[...], recv[DU])).T.astype(BF)

    for a, (_, _, out) in enumerate(big):
        started[a][4].wait_recv()
        out[0, :, 0:TOK] = (upper[pl.ds(a * 256, 128), :] + ye[a, :, 0:TOK].astype(F32)).astype(BF)
        out[0, :, TOK:] = (upper[pl.ds(a * 256 + 128, 128), :] + ye[a, :, TOK:].astype(F32)).astype(BF)

    def summed(s):
        await_bytes(rsmall.at[s, pl.ds(0, NDP - 1)], small_recv.at[s])
        v = rsmall[s, 0].astype(F32)
        for d in range(1, NDP):
            v = v + rsmall[s, d].astype(F32)
        return v.astype(BF)

    ld_o[0] = summed(0)
    for s, out in ((1, rg_o), (2, ru_o)):
        v = summed(s)
        out[0, 0:128, :] = v[:, 0:128]
        out[0, 128:256, :] = v[:, 128:256]

    for i in range(6):
        await_bytes(send.at[i, pl.ds(0, MB - KW)], a2a_send.at[i])
    for a in range(3):
        for cp in started[a]:
            cp.wait_send()
    for s in range(3):
        await_bytes(small.at[s, pl.ds(0, NDP - 1)], small_send.at[s])


def per_device(tokens, gate_in, gate_out, up_in, up_out, down_in, down_out, cotangent):
    anyw = pl.BlockSpec(memory_space=pl.ANY)
    vmem = pl.BlockSpec(memory_space=pltpu.VMEM)
    out_shape = (
        jax.ShapeDtypeStruct((TOK, DB), BF),
        jax.ShapeDtypeStruct((TOK, DB), BF),
        jax.ShapeDtypeStruct((1, DB, 128), BF),
        jax.ShapeDtypeStruct((1, 128, MB), BF),
        jax.ShapeDtypeStruct((1, DB, 128), BF),
        jax.ShapeDtypeStruct((1, 128, MB), BF),
        jax.ShapeDtypeStruct((1, 128, MB), BF),
        jax.ShapeDtypeStruct((1, 128, DB), BF),
    )
    V = pltpu.VMEM
    scratch = [
        V((TOK, DB), BF), V((DB, MB), BF), V((MB, MB), BF), V((DB, MB), BF), V((MB, MB), BF),
        V((MB, MB), BF), V((MB, DB), BF), V((TOK, DB), BF),
        V((DB, TOK), BF), V((MB, MB), BF), V((MB, MB), BF), V((MB, MB), BF), V((DB, MB), BF),
        V((6, MB, TOK), BF), V((6, MB, TOK), BF),
        V((MB, TOK), F32), V((MB, TOK), F32), V((MB, TOK), BF), V((MB, TOK), BF), V((MB, TOK), BF),
        V((DB, TOK), F32),
        V((3, 2, 128, MB), BF), V((3, 2, 128, MB), BF), V((3, 2, 128, MB), BF), V((3, 128, MB), BF),
        V((3, 128, MB), BF), V((3, 128, MB), BF), V((3, 2, 128, MB), BF), V((3, 2, 128, MB), BF), V((3, 128, MB), BF),
        V((3, NDP, 128, DB), BF), V((3, NDP, 128, DB), BF),
        pltpu.SemaphoreType.DMA((8,)), pltpu.SemaphoreType.DMA((6,)), pltpu.SemaphoreType.DMA((6,)),
        pltpu.SemaphoreType.DMA((15,)), pltpu.SemaphoreType.DMA((15,)),
        pltpu.SemaphoreType.DMA((3,)), pltpu.SemaphoreType.DMA((3,)),
    ]
    return pl.pallas_call(
        kernel,
        out_shape=out_shape,
        in_specs=[anyw] * 8,
        out_specs=(vmem,) * 8,
        scratch_shapes=scratch,
        compiler_params=pltpu.CompilerParams(
            collective_id=0, has_side_effects=True, vmem_limit_bytes=60 * 2**20
        ),
        cost_estimate=pl.CostEstimate(flops=12_000_000_000, bytes_accessed=10_000_000, transcendentals=1_000_000),
    )(tokens, gate_in, gate_out, up_in, up_out, down_in, down_out, cotangent)


def solution(mesh):
    in_specs = (
        P("dp", "tensor"),
        P("tensor", None, None),
        P("tensor", None, None),
        P("tensor", None, None),
        P("tensor", None, None),
        P("tensor", None, None),
        P("tensor", None, None),
        P("dp", "tensor"),
    )
    out_specs = (
        P("dp", "tensor"),
        P("dp", "tensor"),
        P("tensor", None, "dp"),
        P("tensor", "dp", None),
        P("tensor", None, "dp"),
        P("tensor", "dp", None),
        P("tensor", "dp", None),
        P("tensor", "dp", None),
    )
    return jax.shard_map(
        per_device, mesh=mesh, in_specs=in_specs, out_specs=out_specs, check_vma=False
    )
```

time: 514 us -> 182 us (0.35)
  waiting for transfers between devices: 381 us -> 0 us
  Pallas kernels: 0 us -> 170 us
  matrix products: 56.9 us -> 0 us
  starting transfers between devices: 46.1 us -> 0 us
  between operations: 14.2 us -> 0.66 us
    reduce_scatter x6 -> x0, waiting for transfers between devices: 245 us -> none  [the longest x1 59.6 us: per_device(): lax.psum_scatter(part_lg.astype(jnp.bfloat16), 'dp', scatter_dimension=1,...]
    pallas_call x0 -> x1, Pallas kernels: none -> 170 us  [per_device(): pl.pallas_call(kernel, out_shape=out_shape, in_specs=[anyw] * 8, out_spec...]
    all_to_all x6 -> x0, waiting for transfers between devices: 136 us -> none  [the longest x1 25.4 us: per_device(): lax.all_to_all(gmid, 'tensor', split_axis=0, concat_axis=1, tiled=True)]
    dot_general x17 -> x0, matrix products: 53.7 us -> none  [mult(): return jnp.einsum(form, left, right, preferred_element_type=jnp.float32)]
    all_to_all x6 -> x0, starting transfers between devices: 45.8 us -> none  [the longest x1 12.8 us: per_device(): lax.all_to_all(umid, 'tensor', split_axis=0, concat_axis=1, tiled=True)]
    unnamed x21 -> x12, local copies, waits for them, and re-layouts: 12.6 us -> 11 us
  transfers between devices with their start and end apart: 12 -> 0, of which waited for: 11 -> 0; matrix products, arithmetic and copies ran while one was open for 11% -> 0% of each run, Pallas kernels for 0% -> 0%
where the time goes in v1:
time: 182 us
  Pallas kernels  170 us (93%)
  local copies, waits for them, and re-layouts  11 us (6%)
    pallas_call x1, Pallas kernels, per_device(): pl.pallas_call(kernel, out_shape=out_shape, in_specs=[anyw] * 8, out_spec...  170 us
    unnamed x12, local copies, waits for them, and re-layouts  11 us

profile of v1, /device:TPU:1, one launch (start us, length us, event | category | flops | bytes accessed | tf_op | source)
XLA Modules:
  0.0 181.9 jit_solution(3459049120379529141)
XLA Ops:
  0.6 170.3 %shard_map.143 = (bf16[512,256]{1,0:T(8,128)(2,1)}, bf16[512,256]{1,0:T(8,128)(2,1)}, bf16[1,256,128]{2,1,0:T(8,128)(2,1)}, bf16[1,128,1024]{2,1,0:T(8,128)(2,1)...) custom-call(bf16[512,256]{1,0:T(8,128)(2,1)} %x_h.1, ...), custom_call_target="tpu_custom_call" | custom-call | flops 12000000000 | bytes 10000000 | tf_op jit(solution)/shard_map/pallas_call | solution.py:339
  170.9 0.0 copy-start
  170.9 0.0 copy-start.1
  170.9 1.7 copy.24
  172.6 1.7 copy.25
  174.3 1.5 copy.26
  175.8 1.7 copy.27
  177.5 1.5 copy.28
  178.9 1.7 copy.29
  180.6 0.0 copy-done
  180.6 0.7 copy.30
  181.3 0.0 copy-done.1
  181.3 0.6 copy.31
Async XLA Ops:
  170.9 9.7 %copy-start = (bf16[1,128,1024]{2,1,0:T(8,128)(2,1)S(1)}, bf16[1,128,1024]{2,1,0:T(8,128)(2,1)}, u32[]{:S(2)}) copy-start(bf16[1,128,1024]{2,1,0:T(8,128)(2,1)} %get-tuple-element.22) | copy-start | bytes 786436
  170.9 10.4 %copy-start.1 = (bf16[1,128,256]{2,1,0:T(8,128)(2,1)S(1)}, bf16[1,128,256]{2,1,0:T(8,128)(2,1)}, u32[]{:S(2)}) copy-start(bf16[1,128,256]{2,1,0:T(8,128)(2,1)} %get-tuple-element.23) | copy-start | bytes 196612

commit v2 on v1

v2 whole, which is shorter than its diff:
```python
import jax
import jax.numpy as jnp
from jax import lax
from jax.experimental import pallas as pl
from jax.experimental.pallas import tpu as pltpu
from jax.sharding import PartitionSpec as P

MESH = pl.DeviceIdType.MESH
BF = jnp.bfloat16
F32 = jnp.float32
NT = (((1,), (1,)), ((), ()))
NN = (((1,), (0,)), ((), ()))
TOK, HALF, DB, MB, KW, NBLK, NDP = 512, 256, 256, 1024, 32, 32, 8


def dot(a, b, form=NN):
    return lax.dot_general(a, b, form, preferred_element_type=F32)


def rows_at(index, size):
    return pl.ds(pl.multiple_of(index * size, size), size)


def tiles(count, body):
    def step(i, carry):
        body(i)
        return carry

    lax.fori_loop(0, count, step, 0)


def kernel(
    x_h, rg_h, lg_h, ru_h, lu_h, rd_h, ld_h, dy_h,
    out_o, dx_o, rg_o, lg_o, ru_o, lu_o, rd_o, ld_o,
    out_v, dx_v, rg_v, lg_v, ru_v, lu_v, rd_v, ld_v,
    xall, wt, wp, ps, rg, lg, ru, lu, rd, ld, dy,
    xt, lgt, lut, rdt, ldt,
    dsend, dd, rdd, send, recv, gum,
    gate, upper, hidden, dgate, dup, dxt,
    p2, pn, pp, ysend, ra, rb, rc, rdn, ye,
    small, rsmall,
    load_sem, store_sem, x_send, z_recv, c_recv, p_send, p_recv, d_send, d_recv, w_send, w_recv,
    a2a_send, a2a_recv, ring_send, ring_recv, small_send, small_recv,
):
    dp, tn = lax.axis_index("dp"), lax.axis_index("tensor")
    xc, yl = dp // 2, dp % 2
    yh, z, core = tn // 16, (tn // 2) % 8, tn % 2

    def block(y, zz, c):
        return (y * 8 + zz) * 2 + c

    def await_bytes(ref, sem):
        pltpu.make_async_copy(ref, ref, sem).wait()

    ring = z * 2 + core
    loads = {}
    for i, (name, src, dst) in enumerate((
        ("rg", rg_h.at[0], rg), ("ru", ru_h.at[0], ru),
        ("x0", x_h.at[pl.ds(0, HALF)], xall.at[0, ring]), ("x1", x_h.at[pl.ds(HALF, HALF)], xall.at[1, ring]),
        ("ld", ld_h.at[0], ld), ("dy", dy_h, dy), ("lg", lg_h.at[0], lg), ("lu", lu_h.at[0], lu), ("rd", rd_h.at[0], rd),
    )):
        loads[name] = pltpu.make_async_copy(src, dst, load_sem.at[i])
        loads[name].start()

    stores = []

    def store(src, dst):
        cp = pltpu.make_async_copy(src, dst, store_sem.at[len(stores)])
        cp.start()
        stores.append(cp)

    def peer(j):
        g = j // 4
        dz = 4 + (1 - 2 * (g % 2)) * ((g + 1) // 2)
        return block((yh + 1 - (j // 2) % 2) % 2, (z + dz) % 8, (core + 1 - j % 2) % 2)

    def dp_peer(j):
        return (dp + 1 + j) % NDP

    barrier = pltpu.get_barrier_semaphore()

    def greet_tensor(j):
        pl.semaphore_signal(barrier, inc=1, device_id=(dp, peer(j)), device_id_type=MESH)

    def greet_dp(j):
        pl.semaphore_signal(barrier, inc=1, device_id=(dp_peer(j), tn), device_id_type=MESH)

    tiles(NBLK - 1, greet_tensor)
    tiles(NDP - 1, greet_dp)

    OFFS = ((0, -1, 1, -2, 2, -3, 3, -4), (0, -1, 1, -2, 2, -3, 3, 4))

    def x_copy(h, b, sem, to):
        pltpu.make_async_remote_copy(
            src_ref=xall.at[h, b], dst_ref=xall.at[h, b], send_sem=x_send.at[h], recv_sem=sem,
            device_id=(dp, to), device_id_type=MESH,
        ).start()

    up_z, down_z = block(yh, (z + 1) % 8, core), block(yh, (z + 7) % 8, core)
    over_y, sibling = block(1 - yh, z, core), block(yh, z, 1 - core)

    def z_event(h, k):
        off = OFFS[h][k]
        b = ((z + off) % 8) * 2 + core
        if k:
            await_bytes(xall.at[h, b], z_recv.at[h, k])
        for sign, to in ((-1, up_z), (1, down_z)):
            if (off == 0 or off * sign > 0) and off + sign in OFFS[h]:
                x_copy(h, b, z_recv.at[h, OFFS[h].index(off + sign)], to)
        x_copy(h, b, c_recv.at[h, k], sibling)

    def flip(src, dst, across, r):
        def body(c):
            dst[rows_at(c, 256), pl.ds(r * 256, 256)] = src[pl.ds(r * 256, 256), rows_at(c, 256)].T

        tiles(across, body)

    def exchange(i, sem, *hs):
        mine = rows_at(tn, KW)

        def one(j):
            to = peer(j)
            pltpu.make_async_remote_copy(
                src_ref=send.at[(i, *hs, rows_at(to, KW))], dst_ref=recv.at[(i, *hs, mine)],
                send_sem=a2a_send.at[sem], recv_sem=a2a_recv.at[sem],
                device_id=(dp, to), device_id_type=MESH,
            ).start()

        tiles(NBLK - 1, one)
        recv[(i, *hs, mine)] = send[(i, *hs, mine)]

    BOTH = slice(None)

    def arrived(i, sem, h=BOTH):
        await_bytes(recv.at[i, h, pl.ds(0, MB - KW)], a2a_recv.at[sem])

    DM, DG, DU = range(3)

    loads["rg"].wait()
    loads["ru"].wait()

    @pl.when(xc < 2)
    def _():
        for r in range(4):
            wt[r // 2, pl.ds(r % 2 * 256, 256), :] = rg[:, pl.ds(r * 256, 256)].T

    @pl.when(xc >= 2)
    def _():
        for r in range(4):
            wt[r // 2, pl.ds(r % 2 * 256, 256), :] = ru[:, pl.ds(r * 256, 256)].T

    def w_rows(at):
        return pl.ds(pl.multiple_of(at * KW + (xc % 2) * 16, 16), 16)

    def send_w(j):
        at = (ring + 1 + j) % 16
        pltpu.make_async_remote_copy(
            src_ref=wt.at[:, w_rows(at)], dst_ref=wp.at[xc, ring], send_sem=w_send.at[0], recv_sem=w_recv.at[0],
            device_id=(dp, yh * 16 + at), device_id_type=MESH,
        ).start()

    pl.semaphore_wait(barrier, NBLK - 1 + NDP - 1)
    tiles(15, send_w)
    loads["x0"].wait()
    z_event(0, 0)
    loads["x1"].wait()
    z_event(1, 0)
    wp[xc, ring] = wt[:, w_rows(ring), :]

    loads["dy"].wait()
    loads["ld"].wait()

    def back_down(q):
        rows = rows_at(q, 256)
        for h in range(2):
            toks = dy[h * HALF:(h + 1) * HALF, :]
            dsend[h, rows, :] = dot(ld[pl.ds(pl.multiple_of((1 - yh) * 512 + q * 256, 256), 256), :], toks, NT).astype(BF)
            dd[yh, h, rows, :] = dot(ld[pl.ds(pl.multiple_of(yh * 512 + q * 256, 256), 256), :], toks, NT).astype(BF)

    tiles(2, back_down)
    to_y = pltpu.make_async_remote_copy(
        src_ref=dsend, dst_ref=dd.at[yh], send_sem=d_send.at[0], recv_sem=d_recv.at[0],
        device_id=(dp, over_y), device_id_type=MESH,
    )
    to_y.start()

    def relay():
        to_y.wait_recv()

        def one(j):
            at = (ring + 1 + j) % 16
            pltpu.make_async_remote_copy(
                src_ref=dd.at[:, :, rows_at(at, KW)], dst_ref=rdd.at[:, :, rows_at(ring, KW)],
                send_sem=d_send.at[1], recv_sem=d_recv.at[1], device_id=(dp, yh * 16 + at), device_id_type=MESH,
            ).start()

        tiles(15, one)
        rdd[:, :, rows_at(ring, KW), :] = dd[:, :, rows_at(ring, KW), :]

    loads["lg"].wait()
    for r in range(4):
        flip(lg, lgt, 4, r)

    await_bytes(wp.at[0, pl.ds(0, 15)], w_recv.at[0])

    def share_w(j):
        to = ((xc + 1 + j) % 4) * 2 + yl
        pltpu.make_async_remote_copy(
            src_ref=wp.at[xc], dst_ref=wp.at[xc], send_sem=w_send.at[1], recv_sem=w_recv.at[1],
            device_id=(to, tn), device_id_type=MESH,
        ).start()

    tiles(3, share_w)

    def first(h, *ks):
        for k in ks:
            await_bytes(xall.at[h, 0], c_recv.at[h, k])
            at = (z + OFFS[h][k]) % 8

            def body(c, at=at):
                b = at * 2 + c
                w = jnp.concatenate([wp[p, b, y] for y in (yh, 1 - yh) for p in range(4)], axis=0)
                v = dot(w, xall[h, b], NT).astype(BF)
                own, rows = rows_at(yh * 16 + b, KW), rows_at(b, KW)
                gum[h, 0, own, :] = v[0:32]
                gum[h, 1, own, :] = v[32:64]
                ps[h, 0, rows, :] = v[64:96]
                ps[h, 1, rows, :] = v[96:128]
                pltpu.make_async_remote_copy(
                    src_ref=ps.at[h, :, rows], dst_ref=gum.at[h, :, own], send_sem=p_send.at[h], recv_sem=p_recv.at[h],
                    device_id=(dp, over_y), device_id_type=MESH,
                ).start()

            tiles(2, body)

    def events(h, *ks):
        for k in ks:
            z_event(h, k)

    loads["lu"].wait()
    for r in range(4):
        flip(lu, lut, 4, r)
    events(0, 1, 2)
    events(1, 1, 2)
    loads["rd"].wait()
    for r in range(4):
        flip(rd, rdt, 4, r)
    events(0, 3, 4)
    events(1, 3, 4)
    for h in range(2):
        xt[h] = xall[h, ring].T
    for r in range(4):
        flip(ld, ldt, 1, r)
    await_bytes(wp.at[pl.ds(0, 3)], w_recv.at[1])
    first(0, 0, 1, 2, 3, 4)
    events(0, 5, 6)
    events(1, 5, 6)
    first(0, 5, 6)
    first(1, 0, 1, 2)
    events(0, 7)
    events(1, 7)
    relay()
    first(0, 7)
    first(1, 3, 4, 5, 6, 7)

    def forward(h):
        await_bytes(gum.at[h, :, pl.ds(0, 512)], p_recv.at[h])

        def body(q):
            rows = rows_at(q, 256)
            g = dot(lgt[rows, :], gum[h, 0])
            u = dot(lut[rows, :], gum[h, 1])
            gate[h, rows, :] = g
            upper[h, rows, :] = u
            hidden[h, rows, :] = (g * jax.nn.sigmoid(g) * u).astype(BF)

        tiles(4, body)

        def down(q):
            rows = rows_at(q, 256)
            send[DM, h, rows, :] = dot(rdt[rows, :], hidden[h]).astype(BF)

        tiles(4, down)
        exchange(DM, h, h)

    forward(0)
    forward(1)
    await_bytes(rdd.at[:, :, pl.ds(0, 480)], d_recv.at[1])

    def backward(h):
        def body(q):
            rows = rows_at(q, 256)
            dh = dot(rd[rows, 0:512], rdd[0, h]) + dot(rd[rows, 512:1024], rdd[1, h])
            g, u = gate[h, rows, :], upper[h, rows, :]
            s = jax.nn.sigmoid(g)
            dgate[h, rows, :] = (dh * u * s * (1.0 + g * (1.0 - s))).astype(BF)
            dup[h, rows, :] = (dh * (g * s)).astype(BF)

        tiles(4, body)

    def mids(i, sem, w, d):
        def body(q):
            rows = rows_at(q, 256)
            for h in range(2):
                send[i, h, rows, :] = dot(w[rows, :], d[h]).astype(BF)

        tiles(4, body)
        exchange(i, sem, BOTH)

    backward(0)
    backward(1)
    mids(DG, 2, lg, dgate)
    mids(DU, 3, lu, dup)

    nxt, prv, opp = (xc + 1) % 4, (xc + 3) % 4, (xc + 2) % 4

    def ship(src, dst, sem, to):
        cp = pltpu.make_async_remote_copy(
            src_ref=src, dst_ref=dst, send_sem=ring_send.at[sem], recv_sem=ring_recv.at[sem],
            device_id=to, device_id_type=MESH,
        )
        cp.start()
        return cp

    to_next, to_prev = (nxt * 2 + yl, tn), (prv * 2 + yl, tn)
    to_pair = (xc * 2 + 1 - yl, tn)
    big = (
        (hidden, rdd, rd_v, rd_o),
        (gum.at[:, 0], dgate, lg_v, lg_o),
        (gum.at[:, 1], dup, lu_v, lu_o),
    )

    def part(left, right, q, half):
        rows = pl.ds(pl.multiple_of(q * 256 + half * 128, 128), 128)

        def both(pick):
            return dot(left[0, rows, :], pick(0), NT) + dot(left[1, rows, :], pick(1), NT)

        if right is rdd:
            return jnp.concatenate([both(lambda h, y=y: rdd[y, h]) for y in range(2)], axis=1)
        return both(lambda h: right[h])

    def quarter(left, right, q, put):
        tiles(2, lambda half: put(half, part(left, right, q, half)))

    started = [[None] * 5 for _ in big]
    for a, (left, right, _, _) in enumerate(big):
        def put(half, v, a=a):
            p2[a, half] = v.astype(BF)

        quarter(left, right, opp, put)
        started[a][0] = ship(p2.at[a, 0], ra.at[a], 5 * a, to_next)
        started[a][1] = ship(p2.at[a, 1], rb.at[a], 5 * a + 1, to_prev)
    for a, (left, right, _, _) in enumerate(big):
        def put_n(half, v, a=a):
            pn[a, half] = v.astype(BF)

        def put_p(half, v, a=a):
            pp[a, half] = v.astype(BF)

        quarter(left, right, nxt, put_n)
        started[a][0].wait_recv()
        pn[a, 0] = (pn[a, 0].astype(F32) + ra[a].astype(F32)).astype(BF)
        started[a][2] = ship(pn.at[a], rc.at[a], 5 * a + 2, to_next)
        quarter(left, right, prv, put_p)
        started[a][1].wait_recv()
        pp[a, 1] = (pp[a, 1].astype(F32) + rb[a].astype(F32)).astype(BF)
        started[a][3] = ship(pp.at[a], rdn.at[a], 5 * a + 3, to_prev)

    def kept(a, c):
        return c % 2, pl.ds((a * 2 + c // 2) * 128, 128)

    for a, (left, right, _, _) in enumerate(big):
        started[a][2].wait_recv()
        started[a][3].wait_recv()

        def total(half, a=a, left=left, right=right):
            return part(left, right, xc, half) + rc[a, half].astype(F32) + rdn[a, half].astype(F32)

        ysend[a] = total(1 - yl).astype(BF)
        started[a][4] = ship(ysend.at[a], ye.at[a], 5 * a + 4, to_pair)
        own = total(yl)
        for c in range(4):
            s, rows = kept(a, c)
            upper[s, rows, :] = own[:, c * 256:(c + 1) * 256]

    def scatter(s):
        def one(j):
            to = dp_peer(j)
            pltpu.make_async_remote_copy(
                src_ref=small.at[s, to], dst_ref=rsmall.at[s, dp],
                send_sem=small_send.at[s], recv_sem=small_recv.at[s],
                device_id=(to, tn), device_id_type=MESH,
            ).start()

        tiles(NDP - 1, one)
        rsmall[s, dp] = small[s, dp]

    arrived(DM, 0, 0)
    arrived(DM, 1, 1)

    def part_ld(d):
        rows = rows_at(d, 128)
        v = dot(recv[DM, 0, rows, :], dy[0:HALF, :]) + dot(recv[DM, 1, rows, :], dy[HALF:, :])
        small[0, d, :, :] = v.astype(BF)

    tiles(NDP, part_ld)
    scatter(0)
    for h in range(2):
        out_v[h * HALF:(h + 1) * HALF, :] = dot(ldt[...], recv[DM, h]).T.astype(BF)
    store(out_v, out_o)

    def part_in(s, i):
        def body(q):
            rows = rows_at(q, 256)
            v = (dot(xt[0], recv[i, 0, rows, :], NT) + dot(xt[1], recv[i, 1, rows, :], NT)).astype(BF)
            small[s, 2 * q, :, :] = jnp.concatenate([v[0:128, 0:128], v[128:256, 0:128]], axis=1)
            small[s, 2 * q + 1, :, :] = jnp.concatenate([v[0:128, 128:256], v[128:256, 128:256]], axis=1)

        tiles(4, body)
        scatter(s)

    arrived(DG, 2)
    part_in(1, DG)
    for h in range(2):
        dxt[h] = dot(rg[...], recv[DG, h])
    for a, (_, _, out, out_h) in enumerate(big):
        started[a][4].wait_recv()
        for c in range(4):
            s, rows = kept(a, c)
            cols = slice(c * 256, (c + 1) * 256)
            out[:, cols] = (upper[s, rows, :] + ye[a, :, cols].astype(F32)).astype(BF)
        store(out, out_h.at[0])

    arrived(DU, 3)
    part_in(2, DU)
    for h in range(2):
        dx_v[h * HALF:(h + 1) * HALF, :] = (dxt[h] + dot(ru[...], recv[DU, h])).T.astype(BF)
    store(dx_v, dx_o)

    def summed(s):
        await_bytes(rsmall.at[s, pl.ds(0, NDP - 1)], small_recv.at[s])
        v = rsmall[s, 0].astype(F32)
        for d in range(1, NDP):
            v = v + rsmall[s, d].astype(F32)
        return v.astype(BF)

    ld_v[...] = summed(0)
    store(ld_v, ld_o.at[0])
    for s, out, out_h in ((1, rg_v, rg_o), (2, ru_v, ru_o)):
        v = summed(s)
        out[0:128, :] = v[:, 0:128]
        out[128:256, :] = v[:, 128:256]
        store(out, out_h.at[0])

    for h in range(2):
        await_bytes(xall.at[h, pl.ds(0, 15)], x_send.at[h])
        await_bytes(ps.at[h], p_send.at[h])
        await_bytes(send.at[DM, h, pl.ds(0, MB - KW)], a2a_send.at[h])
    to_y.wait_send()
    await_bytes(rdd.at[:, :, pl.ds(0, 480)], d_send.at[1])
    for i, sem in ((DG, 2), (DU, 3)):
        await_bytes(send.at[i, :, pl.ds(0, MB - KW)], a2a_send.at[sem])
    await_bytes(wp.at[0, pl.ds(0, 15)], w_send.at[0])
    await_bytes(wp.at[pl.ds(0, 3)], w_send.at[1])
    for a in range(3):
        for cp in started[a]:
            cp.wait_send()
    for s in range(3):
        await_bytes(small.at[s, pl.ds(0, NDP - 1)], small_send.at[s])
    for cp in stores:
        cp.wait()


def hand_over(*refs):
    src, dst, held, (sem,) = refs[:8], refs[8:16], refs[16:24], refs[24:]
    arriving = [pltpu.make_async_copy(src[i], held[i], sem.at[0, i]) for i in range(8)]
    leaving = [pltpu.make_async_copy(held[i], dst[i], sem.at[1, i]) for i in range(8)]
    for cp in arriving:
        cp.start()
    for i in range(8):
        arriving[i].wait()
        leaving[i].start()
    for cp in leaving:
        cp.wait()


def per_device(tokens, gate_in, gate_out, up_in, up_out, down_in, down_out, cotangent):
    anyw = pl.BlockSpec(memory_space=pl.ANY)
    out_shape = (
        jax.ShapeDtypeStruct((TOK, DB), BF),
        jax.ShapeDtypeStruct((TOK, DB), BF),
        jax.ShapeDtypeStruct((1, DB, 128), BF),
        jax.ShapeDtypeStruct((1, 128, MB), BF),
        jax.ShapeDtypeStruct((1, DB, 128), BF),
        jax.ShapeDtypeStruct((1, 128, MB), BF),
        jax.ShapeDtypeStruct((1, 128, MB), BF),
        jax.ShapeDtypeStruct((1, 128, DB), BF),
    )
    V = pltpu.VMEM
    mids = V((2, MB, HALF), BF)
    wide = V((2, MB, HALF), F32)
    square = V((MB, MB), BF)
    dma = pltpu.SemaphoreType.DMA
    scratch = [
        V((TOK, DB), BF), V((TOK, DB), BF), V((DB, 128), BF), V((128, MB), BF),
        V((DB, 128), BF), V((128, MB), BF), V((128, MB), BF), V((128, DB), BF),
        V((2, 16, HALF, DB), BF), V((2, 512, DB), BF), V((4, 16, 2, 16, DB), BF), V((2, 2, 512, HALF), BF),
        V((DB, MB), BF), square, V((DB, MB), BF), square, square, V((MB, DB), BF), V((TOK, DB), BF),
        V((2, DB, HALF), BF), square, square, square, V((DB, MB), BF),
        V((2, 512, HALF), BF), V((2, 2, 512, HALF), BF), V((2, 2, 512, HALF), BF),
        V((3, 2, MB, HALF), BF), V((3, 2, MB, HALF), BF), V((2, 2, MB, HALF), BF),
        wide, wide, mids, mids, mids, V((2, DB, HALF), F32),
        V((3, 2, 128, MB), BF), V((3, 2, 128, MB), BF), V((3, 2, 128, MB), BF), V((3, 128, MB), BF),
        V((3, 128, MB), BF), V((3, 128, MB), BF), V((3, 2, 128, MB), BF), V((3, 2, 128, MB), BF), V((3, 128, MB), BF),
        V((3, NDP, 128, DB), BF), V((3, NDP, 128, DB), BF),
        dma((9,)), dma((8,)), dma((2,)), dma((2, 8)), dma((2, 8)), dma((2,)), dma((2,)), dma((2,)), dma((2,)), dma((2,)), dma((2,)),
        dma((4,)), dma((4,)), dma((15,)), dma((15,)), dma((3,)), dma((3,)),
    ]
    results = pl.pallas_call(
        kernel,
        out_shape=out_shape,
        in_specs=[anyw] * 8,
        out_specs=(anyw,) * 8,
        scratch_shapes=scratch,
        compiler_params=pltpu.CompilerParams(
            collective_id=0, has_side_effects=True, vmem_limit_bytes=62 * 2**20
        ),
        cost_estimate=pl.CostEstimate(flops=12_000_000_000, bytes_accessed=10_000_000, transcendentals=1_000_000),
    )(tokens, gate_in, gate_out, up_in, up_out, down_in, down_out, cotangent)
    return pl.pallas_call(
        hand_over,
        out_shape=out_shape,
        in_specs=[anyw] * 8,
        out_specs=(anyw,) * 8,
        scratch_shapes=[V(o.shape, BF) for o in out_shape] + [pltpu.SemaphoreType.DMA((2, 8))],
    )(*results)


def solution(mesh):
    in_specs = (
        P("dp", "tensor"),
        P("tensor", None, None),
        P("tensor", None, None),
        P("tensor", None, None),
        P("tensor", None, None),
        P("tensor", None, None),
        P("tensor", None, None),
        P("dp", "tensor"),
    )
    out_specs = (
        P("dp", "tensor"),
        P("dp", "tensor"),
        P("tensor", None, "dp"),
        P("tensor", "dp", None),
        P("tensor", None, "dp"),
        P("tensor", "dp", None),
        P("tensor", "dp", None),
        P("tensor", "dp", None),
    )
    return jax.shard_map(
        per_device, mesh=mesh, in_specs=in_specs, out_specs=out_specs, check_vma=False
    )
```

time: 182 us -> 162 us (0.89)
  local copies, waits for them, and re-layouts: 11 us -> 0 us
  Pallas kernels: 170 us -> 160 us
    pallas_call x1, Pallas kernels: 170 us -> 158 us  [per_device(): pl.pallas_call(kernel, out_shape=out_shape, in_specs=[anyw] * 8, out_spec...]
    unnamed x12 -> x0, local copies, waits for them, and re-layouts: 11 us -> none
    pallas_call x0 -> x1, Pallas kernels: none -> 2.2 us  [per_device(): pl.pallas_call(hand_over, out_shape=out_shape, in_specs=[anyw] * 8, out_s...]
where the time goes in v2:
time: 162 us; the launch traced here: 161 us
  Pallas kernels  160 us (99%)
    pallas_call x1, Pallas kernels, per_device(): pl.pallas_call(kernel, out_shape=out_shape, in_specs=[anyw] * 8, out_spec...  158 us

profile of v2, /device:TPU:1, one launch (start us, length us, event | category | flops | bytes accessed | tf_op | source)
XLA Modules:
  0.0 160.7 jit_solution(8040674659498068495)
XLA Ops:
  0.6 157.9 %shard_map.143 = (bf16[512,256]{1,0:T(8,128)(2,1)}, bf16[512,256]{1,0:T(8,128)(2,1)}, bf16[1,256,128]{2,1,0:T(8,128)(2,1)}, bf16[1,128,1024]{2,1,0:T(8,128)(2,1)...) custom-call(bf16[512,256]{1,0:T(8,128)(2,1)} %x_h.1, ...), custom_call_target="tpu_custom_call" | custom-call | flops 12000000000 | bytes 10000000 | tf_op jit(solution)/shard_map/pallas_call | solution.py:520
  158.6 2.2 %shard_map.144 = (bf16[512,256]{1,0:T(8,128)(2,1)}, bf16[512,256]{1,0:T(8,128)(2,1)}, bf16[1,256,128]{2,1,0:T(8,128)(2,1)}, bf16[1,128,1024]{2,1,0:T(8,128)(2,1)...) custom-call(bf16[512,256]{1,0:T(8,128)(2,1)} %get-tuple-element.16.r, ...), custom_call_target="tpu_custom_call" | custom-call | tf_op jit(solution)/shard_map/pallas_call | solution.py:531

commit v3 on v2

--- a/solution.py
+++ b/solution.py
@@ -10,6 +10,7 @@
 F32 = jnp.float32
 NT = (((1,), (1,)), ((), ()))
 NN = (((1,), (0,)), ((), ()))
+TN = (((0,), (0,)), ((), ()))
 TOK, HALF, DB, MB, KW, NBLK, NDP = 512, 256, 256, 1024, 32, 32, 8
 
 
@@ -34,13 +35,14 @@
     out_o, dx_o, rg_o, lg_o, ru_o, lu_o, rd_o, ld_o,
     out_v, dx_v, rg_v, lg_v, ru_v, lu_v, rd_v, ld_v,
     xall, wt, wp, ps, rg, lg, ru, lu, rd, ld, dy,
-    xt, lgt, lut, rdt, ldt,
-    dsend, dd, rdd, send, recv, gum,
-    gate, upper, hidden, dgate, dup, dxt,
+    lgt, lut, rdt, ldt,
+    dsend, dd, rdd, msend, dm, rdm, gum, back, sums_in, chain_in,
+    gate, upper, hidden, dgate, dup,
     p2, pn, pp, ysend, ra, rb, rc, rdn, ye,
-    small, rsmall,
+    wring, lring, wown, lown, wsum, wfin,
     load_sem, store_sem, x_send, z_recv, c_recv, p_send, p_recv, d_send, d_recv, w_send, w_recv,
-    a2a_send, a2a_recv, ring_send, ring_recv, small_send, small_recv,
+    m_send, m_recv, ring_send, ring_recv,
+    b_send, b_recv, s_send, s_recv, ch_send, ch_recv, wf_send, wf_recv,
 ):
     dp, tn = lax.axis_index("dp"), lax.axis_index("tensor")
     xc, yl = dp // 2, dp % 2
@@ -75,7 +77,7 @@
         return block((yh + 1 - (j // 2) % 2) % 2, (z + dz) % 8, (core + 1 - j % 2) % 2)
 
     def dp_peer(j):
-        return (dp + 1 + j) % NDP
+        return (dp + 2 * j + 2) % NDP
 
     barrier = pltpu.get_barrier_semaphore()
 
@@ -86,7 +88,26 @@
         pl.semaphore_signal(barrier, inc=1, device_id=(dp_peer(j), tn), device_id_type=MESH)
 
     tiles(NBLK - 1, greet_tensor)
-    tiles(NDP - 1, greet_dp)
+    tiles(3, greet_dp)
+    pl.semaphore_signal(barrier, inc=1, device_id=(xc * 2 + 1 - yl, tn), device_id_type=MESH)
+
+    def apart(to_dp, to_tn, here, there):
+        same = jnp.logical_and(to_dp == dp, to_tn == tn)
+        pl.when(same)(here)
+        pl.when(jnp.logical_not(same))(there)
+
+    def summed_block(d, par):
+        return ((z + (d if par == 0 else 8 - d)) % 8) * 2 + par
+
+    for j in range(4):
+        away = 8 + z - (2 * (dp % 4) + j // 2)
+        source = ((away * (1 + 6 * core)) % 8, yh * 16 + 4 * (dp % 4) + j)
+
+        def greet_source(source=source):
+            pl.semaphore_signal(barrier, inc=1, device_id=source, device_id_type=MESH)
+
+        apart(*source, lambda: None, greet_source)
+    stays = jnp.logical_and(dp == 0, z < 2).astype(jnp.int32)
 
     OFFS = ((0, -1, 1, -2, 2, -3, 3, -4), (0, -1, 1, -2, 2, -3, 3, 4))
 
@@ -115,27 +136,6 @@
 
         tiles(across, body)
 
-    def exchange(i, sem, *hs):
-        mine = rows_at(tn, KW)
-
-        def one(j):
-            to = peer(j)
-            pltpu.make_async_remote_copy(
-                src_ref=send.at[(i, *hs, rows_at(to, KW))], dst_ref=recv.at[(i, *hs, mine)],
-                send_sem=a2a_send.at[sem], recv_sem=a2a_recv.at[sem],
-                device_id=(dp, to), device_id_type=MESH,
-            ).start()
-
-        tiles(NBLK - 1, one)
-        recv[(i, *hs, mine)] = send[(i, *hs, mine)]
-
-    BOTH = slice(None)
-
-    def arrived(i, sem, h=BOTH):
-        await_bytes(recv.at[i, h, pl.ds(0, MB - KW)], a2a_recv.at[sem])
-
-    DM, DG, DU = range(3)
-
     loads["rg"].wait()
     loads["ru"].wait()
 
@@ -159,7 +159,7 @@
             device_id=(dp, yh * 16 + at), device_id_type=MESH,
         ).start()
 
-    pl.semaphore_wait(barrier, NBLK - 1 + NDP - 1)
+    pl.semaphore_wait(barrier, NBLK - 1 + 3 + 1 + 4 - stays)
     tiles(15, send_w)
     loads["x0"].wait()
     z_event(0, 0)
@@ -184,22 +184,29 @@
     )
     to_y.start()
 
-    def relay():
-        to_y.wait_recv()
-
+    def relay(held, dst, send_sem, recv_sem):
         def one(j):
             at = (ring + 1 + j) % 16
             pltpu.make_async_remote_copy(
-                src_ref=dd.at[:, :, rows_at(at, KW)], dst_ref=rdd.at[:, :, rows_at(ring, KW)],
-                send_sem=d_send.at[1], recv_sem=d_recv.at[1], device_id=(dp, yh * 16 + at), device_id_type=MESH,
+                src_ref=held.at[:, :, rows_at(at, KW)], dst_ref=dst.at[:, :, rows_at(ring, KW)],
+                send_sem=send_sem, recv_sem=recv_sem, device_id=(dp, yh * 16 + at), device_id_type=MESH,
             ).start()
 
         tiles(15, one)
-        rdd[:, :, rows_at(ring, KW), :] = dd[:, :, rows_at(ring, KW), :]
+        dst[:, :, rows_at(ring, KW), :] = held[:, :, rows_at(ring, KW), :]
+
+    def flip_blocks(src, dst):
+        def body(i):
+            r, c = i // 4, i % 4
+            dst[c * 4 + r] = src[rows_at(r, 256), rows_at(c, 256)].T
+
+        tiles(16, body)
+
+    def block_row(t, q):
+        return jnp.concatenate([t[q * 4 + c] for c in range(4)], axis=1)
 
     loads["lg"].wait()
-    for r in range(4):
-        flip(lg, lgt, 4, r)
+    flip_blocks(lg, lgt)
 
     await_bytes(wp.at[0, pl.ds(0, 15)], w_recv.at[0])
 
@@ -212,6 +219,9 @@
 
     tiles(3, share_w)
 
+    def columns(b, *ys):
+        return jnp.concatenate([wp[p, b, y] for y in ys for p in range(4)], axis=0)
+
     def first(h, *ks):
         for k in ks:
             await_bytes(xall.at[h, 0], c_recv.at[h, k])
@@ -219,7 +229,7 @@
 
             def body(c, at=at):
                 b = at * 2 + c
-                w = jnp.concatenate([wp[p, b, y] for y in (yh, 1 - yh) for p in range(4)], axis=0)
+                w = columns(b, yh, 1 - yh)
                 v = dot(w, xall[h, b], NT).astype(BF)
                 own, rows = rows_at(yh * 16 + b, KW), rows_at(b, KW)
                 gum[h, 0, own, :] = v[0:32]
@@ -238,8 +248,7 @@
             z_event(h, k)
 
     loads["lu"].wait()
-    for r in range(4):
-        flip(lu, lut, 4, r)
+    flip_blocks(lu, lut)
     events(0, 1, 2)
     events(1, 1, 2)
     loads["rd"].wait()
@@ -247,8 +256,6 @@
         flip(rd, rdt, 4, r)
     events(0, 3, 4)
     events(1, 3, 4)
-    for h in range(2):
-        xt[h] = xall[h, ring].T
     for r in range(4):
         flip(ld, ldt, 1, r)
     await_bytes(wp.at[pl.ds(0, 3)], w_recv.at[1])
@@ -259,29 +266,43 @@
     first(1, 0, 1, 2)
     events(0, 7)
     events(1, 7)
-    relay()
+    to_y.wait_recv()
+    relay(dd, rdd, d_send.at[1], d_recv.at[1])
     first(0, 7)
     first(1, 3, 4, 5, 6, 7)
 
+    downs = []
+
     def forward(h):
         await_bytes(gum.at[h, :, pl.ds(0, 512)], p_recv.at[h])
 
         def body(q):
             rows = rows_at(q, 256)
-            g = dot(lgt[rows, :], gum[h, 0])
-            u = dot(lut[rows, :], gum[h, 1])
+            g = dot(block_row(lgt, q), gum[h, 0])
+            u = dot(block_row(lut, q), gum[h, 1])
             gate[h, rows, :] = g
             upper[h, rows, :] = u
             hidden[h, rows, :] = (g * jax.nn.sigmoid(g) * u).astype(BF)
 
         tiles(4, body)
 
-        def down(q):
-            rows = rows_at(q, 256)
-            send[DM, h, rows, :] = dot(rdt[rows, :], hidden[h]).astype(BF)
-
-        tiles(4, down)
-        exchange(DM, h, h)
+        def down_over(q):
+            rows = pl.ds(pl.multiple_of((1 - yh) * 512 + q * 256, 256), 256)
+            msend[h, rows_at(q, 256), :] = dot(rdt[rows, :], hidden[h]).astype(BF)
+
+        tiles(2, down_over)
+        cp = pltpu.make_async_remote_copy(
+            src_ref=msend.at[h], dst_ref=dm.at[yh, h], send_sem=m_send.at[h], recv_sem=m_recv.at[h],
+            device_id=(dp, over_y), device_id_type=MESH,
+        )
+        cp.start()
+        downs.append(cp)
+
+        def down_here(q):
+            rows = pl.ds(pl.multiple_of(yh * 512 + q * 256, 256), 256)
+            dm[yh, h, rows_at(q, 256), :] = dot(rdt[rows, :], hidden[h]).astype(BF)
+
+        tiles(2, down_here)
 
     forward(0)
     forward(1)
@@ -298,20 +319,6 @@
 
         tiles(4, body)
 
-    def mids(i, sem, w, d):
-        def body(q):
-            rows = rows_at(q, 256)
-            for h in range(2):
-                send[i, h, rows, :] = dot(w[rows, :], d[h]).astype(BF)
-
-        tiles(4, body)
-        exchange(i, sem, BOTH)
-
-    backward(0)
-    backward(1)
-    mids(DG, 2, lg, dgate)
-    mids(DU, 3, lu, dup)
-
     nxt, prv, opp = (xc + 1) % 4, (xc + 3) % 4, (xc + 2) % 4
 
     def ship(src, dst, sem, to):
@@ -330,144 +337,260 @@
         (gum.at[:, 1], dup, lu_v, lu_o),
     )
 
-    def part(left, right, q, half):
+    def part(a, q, half):
+        if a == 3:
+            return jnp.concatenate([part_in(summed_block(2 * q + half, par)) for par in range(2)], axis=0)
         rows = pl.ds(pl.multiple_of(q * 256 + half * 128, 128), 128)
+        if a == 4:
+            inner = pl.ds(pl.multiple_of(q % 2 * 256 + half * 128, 128), 128)
+            return dot(rdm[q // 2, 0, inner, :], dy[0:HALF, :]) + dot(rdm[q // 2, 1, inner, :], dy[HALF:, :])
+        left, right = big[a][:2]
 
         def both(pick):
             return dot(left[0, rows, :], pick(0), NT) + dot(left[1, rows, :], pick(1), NT)
 
-        if right is rdd:
+        if a == 0:
             return jnp.concatenate([both(lambda h, y=y: rdd[y, h]) for y in range(2)], axis=1)
         return both(lambda h: right[h])
 
-    def quarter(left, right, q, put):
-        tiles(2, lambda half: put(half, part(left, right, q, half)))
-
-    started = [[None] * 5 for _ in big]
-    for a, (left, right, _, _) in enumerate(big):
-        def put(half, v, a=a):
-            p2[a, half] = v.astype(BF)
-
-        quarter(left, right, opp, put)
-        started[a][0] = ship(p2.at[a, 0], ra.at[a], 5 * a, to_next)
-        started[a][1] = ship(p2.at[a, 1], rb.at[a], 5 * a + 1, to_prev)
-    for a, (left, right, _, _) in enumerate(big):
-        def put_n(half, v, a=a):
-            pn[a, half] = v.astype(BF)
-
-        def put_p(half, v, a=a):
-            pp[a, half] = v.astype(BF)
-
-        quarter(left, right, nxt, put_n)
+    started = [[None] * 5 for _ in range(5)]
+    places = [tuple(ref.at[a] for ref in (p2, pn, pp, ysend, ra, rb, rc, rdn, ye)) for a in range(3)]
+    for ref in (wring, lring):
+        places.append(tuple(
+            ref.at[at] if size == 1 else ref.at[pl.ds(at, size)]
+            for at, size in ((0, 2), (2, 2), (4, 2), (6, 1), (7, 1), (8, 1), (9, 2), (11, 2), (13, 1))
+        ))
+
+    def ring1(a):
+        p2, _, _, _, ra, rb = places[a][:6]
+
+        def put(half):
+            p2[half] = part(a, opp, half).astype(BF)
+
+        tiles(2, put)
+        started[a][0] = ship(p2.at[0], ra, 5 * a, to_next)
+        started[a][1] = ship(p2.at[1], rb, 5 * a + 1, to_prev)
+
+    def ring2(a):
+        _, pn, pp, _, ra, rb, rc, rdn, _ = places[a]
+
+        def put_n(half):
+            pn[half] = part(a, nxt, half).astype(BF)
+
+        def put_p(half):
+            pp[half] = part(a, prv, half).astype(BF)
+
+        tiles(2, put_n)
         started[a][0].wait_recv()
-        pn[a, 0] = (pn[a, 0].astype(F32) + ra[a].astype(F32)).astype(BF)
-        started[a][2] = ship(pn.at[a], rc.at[a], 5 * a + 2, to_next)
-        quarter(left, right, prv, put_p)
+        pn[0] = (pn[0].astype(F32) + ra[...].astype(F32)).astype(BF)
+        started[a][2] = ship(pn, rc, 5 * a + 2, to_next)
+        tiles(2, put_p)
         started[a][1].wait_recv()
-        pp[a, 1] = (pp[a, 1].astype(F32) + rb[a].astype(F32)).astype(BF)
-        started[a][3] = ship(pp.at[a], rdn.at[a], 5 * a + 3, to_prev)
+        pp[1] = (pp[1].astype(F32) + rb[...].astype(F32)).astype(BF)
+        started[a][3] = ship(pp, rdn, 5 * a + 3, to_prev)
 
     def kept(a, c):
         return c % 2, pl.ds((a * 2 + c // 2) * 128, 128)
 
-    for a, (left, right, _, _) in enumerate(big):
+    def ring3(a):
+        _, _, _, ysend, _, _, rc, rdn, ye = places[a]
         started[a][2].wait_recv()
         started[a][3].wait_recv()
 
-        def total(half, a=a, left=left, right=right):
-            return part(left, right, xc, half) + rc[a, half].astype(F32) + rdn[a, half].astype(F32)
-
-        ysend[a] = total(1 - yl).astype(BF)
-        started[a][4] = ship(ysend.at[a], ye.at[a], 5 * a + 4, to_pair)
+        def total(half):
+            return part(a, xc, half) + rc[half].astype(F32) + rdn[half].astype(F32)
+
+        ysend[...] = total(1 - yl).astype(BF)
+        started[a][4] = ship(ysend, ye, 5 * a + 4, to_pair)
         own = total(yl)
+        if a >= 3:
+            (wown, lown)[a - 3][...] = own
+            return
         for c in range(4):
             s, rows = kept(a, c)
             upper[s, rows, :] = own[:, c * 256:(c + 1) * 256]
 
-    def scatter(s):
-        def one(j):
-            to = dp_peer(j)
-            pltpu.make_async_remote_copy(
-                src_ref=small.at[s, to], dst_ref=rsmall.at[s, dp],
-                send_sem=small_send.at[s], recv_sem=small_recv.at[s],
-                device_id=(to, tn), device_id_type=MESH,
-            ).start()
-
-        tiles(NDP - 1, one)
-        rsmall[s, dp] = small[s, dp]
-
-    arrived(DM, 0, 0)
-    arrived(DM, 1, 1)
-
-    def part_ld(d):
-        rows = rows_at(d, 128)
-        v = dot(recv[DM, 0, rows, :], dy[0:HALF, :]) + dot(recv[DM, 1, rows, :], dy[HALF:, :])
-        small[0, d, :, :] = v.astype(BF)
-
-    tiles(NDP, part_ld)
-    scatter(0)
-    for h in range(2):
-        out_v[h * HALF:(h + 1) * HALF, :] = dot(ldt[...], recv[DM, h]).T.astype(BF)
-    store(out_v, out_o)
-
-    def part_in(s, i):
-        def body(q):
-            rows = rows_at(q, 256)
-            v = (dot(xt[0], recv[i, 0, rows, :], NT) + dot(xt[1], recv[i, 1, rows, :], NT)).astype(BF)
-            small[s, 2 * q, :, :] = jnp.concatenate([v[0:128, 0:128], v[128:256, 0:128]], axis=1)
-            small[s, 2 * q + 1, :, :] = jnp.concatenate([v[0:128, 128:256], v[128:256, 128:256]], axis=1)
-
-        tiles(4, body)
-        scatter(s)
-
-    arrived(DG, 2)
-    part_in(1, DG)
-    for h in range(2):
-        dxt[h] = dot(rg[...], recv[DG, h])
-    for a, (_, _, out, out_h) in enumerate(big):
+    def ring4(a):
+        ye = places[a][8]
         started[a][4].wait_recv()
+        if a == 3:
+            wsum[...] = (wown[...] + ye[...].astype(F32)).astype(BF)
+            return
+        if a == 4:
+            ld_v[...] = (lown[...] + ye[...].astype(F32)).astype(BF)
+            store(ld_v, ld_o.at[0])
+            return
+        out, out_h = big[a][2:]
         for c in range(4):
             s, rows = kept(a, c)
             cols = slice(c * 256, (c + 1) * 256)
-            out[:, cols] = (upper[s, rows, :] + ye[a, :, cols].astype(F32)).astype(BF)
+            out[:, cols] = (upper[s, rows, :] + ye[:, cols].astype(F32)).astype(BF)
         store(out, out_h.at[0])
 
-    arrived(DU, 3)
-    part_in(2, DU)
     for h in range(2):
-        dx_v[h * HALF:(h + 1) * HALF, :] = (dxt[h] + dot(ru[...], recv[DU, h])).T.astype(BF)
+        await_bytes(ps.at[h], p_send.at[h])
+    crossing = []
+
+    def mids_over(gu, w, d):
+        def body(q):
+            src = pl.ds(pl.multiple_of((1 - yh) * 512 + q * 256, 256), 256)
+            for h in range(2):
+                ps[gu, h, rows_at(q, 256), :] = dot(w[src, :], d[h]).astype(BF)
+
+        tiles(2, body)
+        cp = pltpu.make_async_remote_copy(
+            src_ref=ps.at[gu], dst_ref=back.at[yh, gu], send_sem=b_send.at[gu], recv_sem=b_recv.at[gu],
+            device_id=(dp, over_y), device_id_type=MESH,
+        )
+        cp.start()
+        crossing.append(cp)
+
+    def mids_here(gu, w, d):
+        def body(q):
+            src = pl.ds(pl.multiple_of(yh * 512 + q * 256, 256), 256)
+            for h in range(2):
+                back[yh, gu, h, rows_at(q, 256), :] = dot(w[src, :], d[h]).astype(BF)
+
+        tiles(2, body)
+
+    ring1(0)
+    backward(0)
+    backward(1)
+    mids_over(0, lg, dgate)
+    ring1(1)
+    mids_over(1, lu, dup)
+    ring1(2)
+    for cp in downs:
+        cp.wait_recv()
+    relay(dm, rdm, m_send.at[2], m_recv.at[2])
+    ring2(0)
+    mids_here(0, lg, dgate)
+    mids_here(1, lu, dup)
+    ring2(1)
+
+    await_bytes(rdm.at[:, :, pl.ds(0, 480)], m_recv.at[2])
+    ring1(4)
+    for h in range(2):
+        out_v[h * HALF:(h + 1) * HALF, :] = (
+            dot(ldt[:, 0:512], rdm[0, h]) + dot(ldt[:, 512:], rdm[1, h])
+        ).T.astype(BF)
+    store(out_v, out_o)
+
+    for cp in crossing:
+        cp.wait_recv()
+
+    def stacked(h, b):
+        rows = rows_at(b, KW)
+        return jnp.concatenate([back[y, gu, h, rows, :] for y in range(2) for gu in range(2)], axis=0)
+
+    def dx_part(h, zz, c):
+        b = zz * 2 + c
+        return dot(stacked(h, b), columns(b, 0, 1), TN)
+
+    def for_sibling(d):
+        zz = (z + 4 + d) % 8
+        for h in range(2):
+            lgt[h * 8 + zz] = dx_part(h, zz, 1 - core).astype(BF)
+            pltpu.make_async_remote_copy(
+                src_ref=lgt.at[h * 8 + zz], dst_ref=sums_in.at[h, zz], send_sem=s_send.at[0], recv_sem=s_recv.at[h, d],
+                device_id=(dp, sibling), device_id_type=MESH,
+            ).start()
+
+    for d in range(8):
+        for_sibling(d)
+
+    def slab_sum(h, off):
+        zz = (z + off) % 8
+        await_bytes(sums_in.at[h, zz], s_recv.at[h, (off + 4) % 8])
+        return dx_part(h, zz, core) + sums_in[h, zz].astype(F32)
+
+    REACH = ((4, 3), (3, 4))
+    links = []
+
+    def chain(d):
+        for h in range(2):
+            for way, (sign, to) in enumerate(((1, up_z), (-1, down_z))):
+                far = REACH[h][way]
+                if d > far:
+                    continue
+                v = slab_sum(h, sign * d)
+                if d < far:
+                    await_bytes(chain_in.at[h, way, d], ch_recv.at[h, way, d])
+                    v = v + chain_in[h, way, d].astype(F32)
+                slot = (h * 2 + way) * 4 + d - 1
+                lut[slot] = v.astype(BF)
+                cp = pltpu.make_async_remote_copy(
+                    src_ref=lut.at[slot], dst_ref=chain_in.at[h, way, d - 1],
+                    send_sem=ch_send.at[slot], recv_sem=ch_recv.at[h, way, d - 1],
+                    device_id=(dp, to), device_id_type=MESH,
+                )
+                cp.start()
+                links.append(cp)
+
+    def part_in(b):
+        return dot(stacked(0, b), xall[0, b]) + dot(stacked(1, b), xall[1, b])
+
+    chain(4)
+    ring1(3)
+    chain(3)
+    ring3(0)
+    ring2(3)
+    ring2(2)
+    chain(2)
+    ring3(1)
+    chain(1)
+    ring2(4)
+    ring3(3)
+    for h in range(2):
+        v = slab_sum(h, 0)
+        for way in range(2):
+            await_bytes(chain_in.at[h, way, 0], ch_recv.at[h, way, 0])
+            v = v + chain_in[h, way, 0].astype(F32)
+        dx_v[h * HALF:(h + 1) * HALF, :] = v.astype(BF)
     store(dx_v, dx_o)
-
-    def summed(s):
-        await_bytes(rsmall.at[s, pl.ds(0, NDP - 1)], small_recv.at[s])
-        v = rsmall[s, 0].astype(F32)
-        for d in range(1, NDP):
-            v = v + rsmall[s, d].astype(F32)
-        return v.astype(BF)
-
-    ld_v[...] = summed(0)
-    store(ld_v, ld_o.at[0])
-    for s, out, out_h in ((1, rg_v, rg_o), (2, ru_v, ru_o)):
-        v = summed(s)
-        out[0:128, :] = v[:, 0:128]
-        out[128:256, :] = v[:, 128:256]
+    ring4(0)
+    ring4(1)
+
+    ring4(3)
+    final = []
+    for par in range(2):
+        for cs in range(2):
+            to = (cs * 4 + ring // 4, yh * 16 + summed_block(dp, par))
+            src, dst = wsum.at[pl.ds(par * 128 + cs * 64, 64)], wfin.at[ring % 4]
+            away = pltpu.make_async_remote_copy(
+                src_ref=src, dst_ref=dst, send_sem=wf_send.at[par * 2 + cs], recv_sem=wf_recv.at[0],
+                device_id=to, device_id_type=MESH,
+            )
+
+            def keep(src=src, dst=dst):
+                pltpu.make_async_copy(src, dst, wf_recv.at[0]).start()
+
+            apart(*to, keep, away.start)
+            final.append((to, away))
+    ring3(2)
+    ring3(4)
+    await_bytes(wfin, wf_recv.at[0])
+    for gu, (out, out_h) in enumerate(((rg_v, rg_o), (ru_v, ru_o))):
+        out[...] = jnp.concatenate([wfin[j, gu * KW:(gu + 1) * KW, :] for j in range(4)], axis=0).T
         store(out, out_h.at[0])
+    ring4(2)
+    ring4(4)
 
     for h in range(2):
         await_bytes(xall.at[h, pl.ds(0, 15)], x_send.at[h])
-        await_bytes(ps.at[h], p_send.at[h])
-        await_bytes(send.at[DM, h, pl.ds(0, MB - KW)], a2a_send.at[h])
     to_y.wait_send()
     await_bytes(rdd.at[:, :, pl.ds(0, 480)], d_send.at[1])
-    for i, sem in ((DG, 2), (DU, 3)):
-        await_bytes(send.at[i, :, pl.ds(0, MB - KW)], a2a_send.at[sem])
     await_bytes(wp.at[0, pl.ds(0, 15)], w_send.at[0])
     await_bytes(wp.at[pl.ds(0, 3)], w_send.at[1])
-    for a in range(3):
-        for cp in started[a]:
+    await_bytes(rdm.at[:, :, pl.ds(0, 480)], m_send.at[2])
+    for cp in crossing + links + downs:
+        cp.wait_send()
+    await_bytes(sums_in, s_send.at[0])
+    for group in started:
+        for cp in group:
             cp.wait_send()
-    for s in range(3):
-        await_bytes(small.at[s, pl.ds(0, NDP - 1)], small_send.at[s])
+    for to, away in final:
+        apart(*to, lambda: None, away.wait_send)
     for cp in stores:
         cp.wait()
 
@@ -507,15 +630,18 @@
         V((DB, 128), BF), V((128, MB), BF), V((128, MB), BF), V((128, DB), BF),
         V((2, 16, HALF, DB), BF), V((2, 512, DB), BF), V((4, 16, 2, 16, DB), BF), V((2, 2, 512, HALF), BF),
         V((DB, MB), BF), square, V((DB, MB), BF), square, square, V((MB, DB), BF), V((TOK, DB), BF),
-        V((2, DB, HALF), BF), square, square, square, V((DB, MB), BF),
+        V((16, 256, 256), BF), V((16, 256, 256), BF), square, V((DB, MB), BF),
         V((2, 512, HALF), BF), V((2, 2, 512, HALF), BF), V((2, 2, 512, HALF), BF),
-        V((3, 2, MB, HALF), BF), V((3, 2, MB, HALF), BF), V((2, 2, MB, HALF), BF),
-        wide, wide, mids, mids, mids, V((2, DB, HALF), F32),
+        V((2, 512, HALF), BF), V((2, 2, 512, HALF), BF), V((2, 2, 512, HALF), BF), V((2, 2, MB, HALF), BF),
+        V((2, 2, 2, 512, HALF), BF), V((2, 8, HALF, DB), BF), V((2, 2, 4, HALF, DB), BF),
+        wide, wide, mids, mids, mids,
         V((3, 2, 128, MB), BF), V((3, 2, 128, MB), BF), V((3, 2, 128, MB), BF), V((3, 128, MB), BF),
         V((3, 128, MB), BF), V((3, 128, MB), BF), V((3, 2, 128, MB), BF), V((3, 2, 128, MB), BF), V((3, 128, MB), BF),
-        V((3, NDP, 128, DB), BF), V((3, NDP, 128, DB), BF),
-        dma((9,)), dma((8,)), dma((2,)), dma((2, 8)), dma((2, 8)), dma((2,)), dma((2,)), dma((2,)), dma((2,)), dma((2,)), dma((2,)),
-        dma((4,)), dma((4,)), dma((15,)), dma((15,)), dma((3,)), dma((3,)),
+        V((14, 256, DB), BF), V((14, 128, DB), BF), V((256, DB), F32), V((128, DB), F32), V((256, DB), BF), V((4, 64, DB), BF),
+        dma((9,)), dma((8,)), dma((2,)), dma((2, 8)), dma((2, 8)), dma((2,)), dma((2,)), dma((2,)), dma((2,)),
+        dma((2,)), dma((2,)),
+        dma((3,)), dma((3,)), dma((25,)), dma((25,)),
+        dma((2,)), dma((2,)), dma((1,)), dma((2, 8)), dma((16,)), dma((2, 2, 4)), dma((4,)), dma((1,)),
     ]
     results = pl.pallas_call(
         kernel,

time: 162 us -> 145 us (0.90)
  Pallas kernels: 160 us -> 144 us
    pallas_call x1, Pallas kernels: 158 us -> 142 us  [per_device(): pl.pallas_call(kernel, out_shape=out_shape, in_specs=[anyw] * 8, out_spec...]
where the time goes in v3:
time: 145 us
  Pallas kernels  144 us (99%)
    pallas_call x1, Pallas kernels, per_device(): pl.pallas_call(kernel, out_shape=out_shape, in_specs=[anyw] * 8, out_spec...  142 us

profile of v3, /device:TPU:1, one launch (start us, length us, event | category | flops | bytes accessed | tf_op | source)
XLA Modules:
  0.0 145.1 jit_solution(15869159899657437145)
XLA Ops:
  0.6 142.2 %shard_map.143 = (bf16[512,256]{1,0:T(8,128)(2,1)}, bf16[512,256]{1,0:T(8,128)(2,1)}, bf16[1,256,128]{2,1,0:T(8,128)(2,1)}, bf16[1,128,1024]{2,1,0:T(8,128)(2,1)...) custom-call(bf16[512,256]{1,0:T(8,128)(2,1)} %x_h.1, ...), custom_call_target="tpu_custom_call" | custom-call | flops 12000000000 | bytes 10000000 | tf_op jit(solution)/shard_map/pallas_call | solution.py:646
  142.9 2.2 %shard_map.144 = (bf16[512,256]{1,0:T(8,128)(2,1)}, bf16[512,256]{1,0:T(8,128)(2,1)}, bf16[1,256,128]{2,1,0:T(8,128)(2,1)}, bf16[1,128,1024]{2,1,0:T(8,128)(2,1)...) custom-call(bf16[512,256]{1,0:T(8,128)(2,1)} %get-tuple-element.16.r, ...), custom_call_target="tpu_custom_call" | custom-call | tf_op jit(solution)/shard_map/pallas_call | solution.py:657

commit v4 on v3

--- a/solution.py
+++ b/solution.py
@@ -19,7 +19,8 @@
 
 
 def rows_at(index, size):
-    return pl.ds(pl.multiple_of(index * size, size), size)
+    start = index * size
+    return pl.ds(start if isinstance(start, int) else pl.multiple_of(start, size), size)
 
 
 def tiles(count, body):
@@ -28,6 +29,11 @@
         return carry
 
     lax.fori_loop(0, count, step, 0)
+
+
+def unrolled(count, body):
+    for i in range(count):
+        body(i)
 
 
 def kernel(
@@ -39,9 +45,9 @@
     dsend, dd, rdd, msend, dm, rdm, gum, back, sums_in, chain_in,
     gate, upper, hidden, dgate, dup,
     p2, pn, pp, ysend, ra, rb, rc, rdn, ye,
-    wring, lring, wown, lown, wsum, wfin,
+    wring, lring, wyout, wyin, lown, wsum, wfin,
     load_sem, store_sem, x_send, z_recv, c_recv, p_send, p_recv, d_send, d_recv, w_send, w_recv,
-    m_send, m_recv, ring_send, ring_recv,
+    m_send, m_recv, ring_send, ring_recv, cross_send, cross_recv,
     b_send, b_recv, s_send, s_recv, ch_send, ch_recv, wf_send, wf_recv,
 ):
     dp, tn = lax.axis_index("dp"), lax.axis_index("tensor")
@@ -97,7 +103,7 @@
         pl.when(jnp.logical_not(same))(there)
 
     def summed_block(d, par):
-        return ((z + (d if par == 0 else 8 - d)) % 8) * 2 + par
+        return ((z + d + par * (8 - 2 * d)) % 8) * 2 + par
 
     for j in range(4):
         away = 8 + z - (2 * (dp % 4) + j // 2)
@@ -184,16 +190,17 @@
     )
     to_y.start()
 
-    def relay(held, dst, send_sem, recv_sem):
-        def one(j):
-            at = (ring + 1 + j) % 16
+    HOPS = (8, 7, 9, 6, 10, 5, 11, 12, 4, 13, 3, 14, 2, 15, 1)
+
+    def relay(held, dst, send_sem, recv_sem, start=0, end=15, h=slice(None)):
+        for hop in HOPS[start:end]:
+            at = (ring + hop) % 16
             pltpu.make_async_remote_copy(
-                src_ref=held.at[:, :, rows_at(at, KW)], dst_ref=dst.at[:, :, rows_at(ring, KW)],
+                src_ref=held.at[:, h, rows_at(at, KW)], dst_ref=dst.at[:, h, rows_at(ring, KW)],
                 send_sem=send_sem, recv_sem=recv_sem, device_id=(dp, yh * 16 + at), device_id_type=MESH,
             ).start()
-
-        tiles(15, one)
-        dst[:, :, rows_at(ring, KW), :] = held[:, :, rows_at(ring, KW), :]
+        if end == 15:
+            dst[:, h, rows_at(ring, KW), :] = held[:, h, rows_at(ring, KW), :]
 
     def flip_blocks(src, dst):
         def body(i):
@@ -262,12 +269,13 @@
     first(0, 0, 1, 2, 3, 4)
     events(0, 5, 6)
     events(1, 5, 6)
+    to_y.wait_recv()
+    relay(dd, rdd, d_send.at[1], d_recv.at[1], 0, 4)
     first(0, 5, 6)
     first(1, 0, 1, 2)
     events(0, 7)
     events(1, 7)
-    to_y.wait_recv()
-    relay(dd, rdd, d_send.at[1], d_recv.at[1])
+    relay(dd, rdd, d_send.at[1], d_recv.at[1], 4, 15)
     first(0, 7)
     first(1, 3, 4, 5, 6, 7)
 
@@ -284,13 +292,13 @@
             upper[h, rows, :] = u
             hidden[h, rows, :] = (g * jax.nn.sigmoid(g) * u).astype(BF)
 
-        tiles(4, body)
+        unrolled(4, body)
 
         def down_over(q):
             rows = pl.ds(pl.multiple_of((1 - yh) * 512 + q * 256, 256), 256)
             msend[h, rows_at(q, 256), :] = dot(rdt[rows, :], hidden[h]).astype(BF)
 
-        tiles(2, down_over)
+        unrolled(2, down_over)
         cp = pltpu.make_async_remote_copy(
             src_ref=msend.at[h], dst_ref=dm.at[yh, h], send_sem=m_send.at[h], recv_sem=m_recv.at[h],
             device_id=(dp, over_y), device_id_type=MESH,
@@ -302,7 +310,7 @@
             rows = pl.ds(pl.multiple_of(yh * 512 + q * 256, 256), 256)
             dm[yh, h, rows_at(q, 256), :] = dot(rdt[rows, :], hidden[h]).astype(BF)
 
-        tiles(2, down_here)
+        unrolled(2, down_here)
 
     forward(0)
     forward(1)
@@ -317,7 +325,7 @@
             dgate[h, rows, :] = (dh * u * s * (1.0 + g * (1.0 - s))).astype(BF)
             dup[h, rows, :] = (dh * (g * s)).astype(BF)
 
-        tiles(4, body)
+        unrolled(4, body)
 
     nxt, prv, opp = (xc + 1) % 4, (xc + 3) % 4, (xc + 2) % 4
 
@@ -339,11 +347,14 @@
 
     def part(a, q, half):
         if a == 3:
-            return jnp.concatenate([part_in(summed_block(2 * q + half, par)) for par in range(2)], axis=0)
+            return part_in(summed_block(2 * q + yl, half)) + wyin[q, half].astype(F32)
+        if a == 4:
+            rows = pl.ds(pl.multiple_of(q % 2 * 256 + half * 128, 128), 128)
+            return dot(rdm[q // 2, 0, rows, :], dy[0:HALF, :]) + dot(rdm[q // 2, 1, rows, :], dy[HALF:, :])
         rows = pl.ds(pl.multiple_of(q * 256 + half * 128, 128), 128)
-        if a == 4:
-            inner = pl.ds(pl.multiple_of(q % 2 * 256 + half * 128, 128), 128)
-            return dot(rdm[q // 2, 0, inner, :], dy[0:HALF, :]) + dot(rdm[q // 2, 1, inner, :], dy[HALF:, :])
+        if a in (2, 5):
+            cols = slice(0, 512) if a == 2 else slice(512, 1024)
+            return dot(gum[0, 1, rows, :], dup[0, cols, :], NT) + dot(gum[1, 1, rows, :], dup[1, cols, :], NT)
         left, right = big[a][:2]
 
         def both(pick):
@@ -353,16 +364,39 @@
             return jnp.concatenate([both(lambda h, y=y: rdd[y, h]) for y in range(2)], axis=1)
         return both(lambda h: right[h])
 
-    started = [[None] * 5 for _ in range(5)]
-    places = [tuple(ref.at[a] for ref in (p2, pn, pp, ysend, ra, rb, rc, rdn, ye)) for a in range(3)]
+    started = [[None] * 5 for _ in range(6)]
+    steps = (p2, pn, pp, ysend, ra, rb, rc, rdn, ye)
+    places = [tuple(ref.at[a] for ref in steps) for a in range(2)]
+
+    def columns_of(a):
+        at = pl.ds(0 if a == 2 else 512, 512)
+        return tuple(ref.at[2, :, :, at] if ref.ndim == 4 else ref.at[2, :, at] for ref in steps)
+
+    places.append(columns_of(2))
     for ref in (wring, lring):
         places.append(tuple(
             ref.at[at] if size == 1 else ref.at[pl.ds(at, size)]
             for at, size in ((0, 2), (2, 2), (4, 2), (6, 1), (7, 1), (8, 1), (9, 2), (11, 2), (13, 1))
         ))
+    places.append(columns_of(5))
+
+    crossed = []
+
+    def cross_first():
+        for n, q in enumerate((opp, nxt, prv, xc)):
+            for half in range(2):
+                wyout[q, half] = part_in(summed_block(2 * q + 1 - yl, half)).astype(BF)
+            cp = pltpu.make_async_remote_copy(
+                src_ref=wyout.at[q], dst_ref=wyin.at[q], send_sem=cross_send.at[n], recv_sem=cross_recv.at[n],
+                device_id=to_pair, device_id_type=MESH,
+            )
+            cp.start()
+            crossed.append(cp)
 
     def ring1(a):
         p2, _, _, _, ra, rb = places[a][:6]
+        if a == 3:
+            crossed[0].wait_recv()
 
         def put(half):
             p2[half] = part(a, opp, half).astype(BF)
@@ -373,6 +407,9 @@
 
     def ring2(a):
         _, pn, pp, _, ra, rb, rc, rdn, _ = places[a]
+        if a == 3:
+            crossed[1].wait_recv()
+            crossed[2].wait_recv()
 
         def put_n(half):
             pn[half] = part(a, nxt, half).astype(BF)
@@ -394,90 +431,98 @@
 
     def ring3(a):
         _, _, _, ysend, _, _, rc, rdn, ye = places[a]
+        if a == 3:
+            crossed[3].wait_recv()
         started[a][2].wait_recv()
         started[a][3].wait_recv()
 
         def total(half):
             return part(a, xc, half) + rc[half].astype(F32) + rdn[half].astype(F32)
 
+        if a == 3:
+            for half in range(2):
+                wsum[half * 128:(half + 1) * 128, :] = total(half).astype(BF)
+            return
         ysend[...] = total(1 - yl).astype(BF)
         started[a][4] = ship(ysend, ye, 5 * a + 4, to_pair)
         own = total(yl)
-        if a >= 3:
-            (wown, lown)[a - 3][...] = own
+        if a == 4:
+            lown[...] = own
             return
-        for c in range(4):
-            s, rows = kept(a, c)
-            upper[s, rows, :] = own[:, c * 256:(c + 1) * 256]
+        for c, cols in wide_columns(a):
+            s, rows = kept(min(a, 2), c)
+            upper[s, rows, :] = own[:, cols]
+
+    def wide_columns(a):
+        first = 2 if a == 5 else 0
+        return [(first + c, slice(c * 256, (c + 1) * 256)) for c in range(2 if a in (2, 5) else 4)]
 
     def ring4(a):
         ye = places[a][8]
         started[a][4].wait_recv()
-        if a == 3:
-            wsum[...] = (wown[...] + ye[...].astype(F32)).astype(BF)
-            return
         if a == 4:
             ld_v[...] = (lown[...] + ye[...].astype(F32)).astype(BF)
             store(ld_v, ld_o.at[0])
             return
-        out, out_h = big[a][2:]
-        for c in range(4):
-            s, rows = kept(a, c)
-            cols = slice(c * 256, (c + 1) * 256)
-            out[:, cols] = (upper[s, rows, :] + ye[:, cols].astype(F32)).astype(BF)
-        store(out, out_h.at[0])
+        out, out_h = big[min(a, 2)][2:]
+        for c, cols in wide_columns(a):
+            s, rows = kept(min(a, 2), c)
+            out[:, c * 256:(c + 1) * 256] = (upper[s, rows, :] + ye[:, cols].astype(F32)).astype(BF)
+        if a != 2:
+            store(out, out_h.at[0])
 
     for h in range(2):
         await_bytes(ps.at[h], p_send.at[h])
     crossing = []
 
-    def mids_over(gu, w, d):
-        def body(q):
+    def mids_over(gu, h):
+        w, d = ((lg, dgate), (lu, dup))[gu]
+        for q in range(2):
             src = pl.ds(pl.multiple_of((1 - yh) * 512 + q * 256, 256), 256)
-            for h in range(2):
-                ps[gu, h, rows_at(q, 256), :] = dot(w[src, :], d[h]).astype(BF)
-
-        tiles(2, body)
+            ps[gu, h, q * 256:(q + 1) * 256, :] = dot(w[src, :], d[h]).astype(BF)
         cp = pltpu.make_async_remote_copy(
-            src_ref=ps.at[gu], dst_ref=back.at[yh, gu], send_sem=b_send.at[gu], recv_sem=b_recv.at[gu],
+            src_ref=ps.at[gu, h], dst_ref=back.at[yh, gu, h], send_sem=b_send.at[gu * 2 + h], recv_sem=b_recv.at[gu * 2 + h],
             device_id=(dp, over_y), device_id_type=MESH,
         )
         cp.start()
         crossing.append(cp)
 
-    def mids_here(gu, w, d):
-        def body(q):
+    def mids_here(gu, h):
+        w, d = ((lg, dgate), (lu, dup))[gu]
+        for q in range(2):
             src = pl.ds(pl.multiple_of(yh * 512 + q * 256, 256), 256)
-            for h in range(2):
-                back[yh, gu, h, rows_at(q, 256), :] = dot(w[src, :], d[h]).astype(BF)
-
-        tiles(2, body)
-
+            back[yh, gu, h, q * 256:(q + 1) * 256, :] = dot(w[src, :], d[h]).astype(BF)
+
+    downs[0].wait_recv()
+    relay(dm, rdm, m_send.at[2], m_recv.at[2], 0, 15, 0)
     ring1(0)
     backward(0)
+    mids_over(0, 0)
+    mids_over(1, 0)
     backward(1)
-    mids_over(0, lg, dgate)
+    mids_over(0, 1)
+    mids_over(1, 1)
     ring1(1)
-    mids_over(1, lu, dup)
+    downs[1].wait_recv()
+    relay(dm, rdm, m_send.at[3], m_recv.at[3], 0, 7, 1)
     ring1(2)
-    for cp in downs:
-        cp.wait_recv()
-    relay(dm, rdm, m_send.at[2], m_recv.at[2])
+    ring1(5)
+    mids_here(0, 0)
+    mids_here(1, 0)
     ring2(0)
-    mids_here(0, lg, dgate)
-    mids_here(1, lu, dup)
+    mids_here(0, 1)
+    mids_here(1, 1)
     ring2(1)
 
-    await_bytes(rdm.at[:, :, pl.ds(0, 480)], m_recv.at[2])
-    ring1(4)
-    for h in range(2):
-        out_v[h * HALF:(h + 1) * HALF, :] = (
-            dot(ldt[:, 0:512], rdm[0, h]) + dot(ldt[:, 512:], rdm[1, h])
-        ).T.astype(BF)
-    store(out_v, out_o)
-
-    for cp in crossing:
-        cp.wait_recv()
+    def outputs():
+        for h in range(2):
+            await_bytes(rdm.at[:, h, pl.ds(0, 480)], m_recv.at[2 + h])
+        ring1(4)
+        for h in range(2):
+            out_v[h * HALF:(h + 1) * HALF, :] = (
+                dot(ldt[:, 0:512], rdm[0, h]) + dot(ldt[:, 512:], rdm[1, h])
+            ).T.astype(BF)
+        store(out_v, out_o)
 
     def stacked(h, b):
         rows = rows_at(b, KW)
@@ -487,18 +532,17 @@
         b = zz * 2 + c
         return dot(stacked(h, b), columns(b, 0, 1), TN)
 
-    def for_sibling(d):
-        zz = (z + 4 + d) % 8
-        for h in range(2):
+    def for_sibling(h):
+        for cp in crossing[2 * h:2 * h + 2]:
+            cp.wait_recv()
+        for d in range(8):
+            zz = (z + 4 + d) % 8
             lgt[h * 8 + zz] = dx_part(h, zz, 1 - core).astype(BF)
             pltpu.make_async_remote_copy(
                 src_ref=lgt.at[h * 8 + zz], dst_ref=sums_in.at[h, zz], send_sem=s_send.at[0], recv_sem=s_recv.at[h, d],
                 device_id=(dp, sibling), device_id_type=MESH,
             ).start()
 
-    for d in range(8):
-        for_sibling(d)
-
     def slab_sum(h, off):
         zz = (z + off) % 8
         await_bytes(sums_in.at[h, zz], s_recv.at[h, (off + 4) % 8])
@@ -507,51 +551,55 @@
     REACH = ((4, 3), (3, 4))
     links = []
 
-    def chain(d):
-        for h in range(2):
-            for way, (sign, to) in enumerate(((1, up_z), (-1, down_z))):
-                far = REACH[h][way]
-                if d > far:
-                    continue
-                v = slab_sum(h, sign * d)
-                if d < far:
-                    await_bytes(chain_in.at[h, way, d], ch_recv.at[h, way, d])
-                    v = v + chain_in[h, way, d].astype(F32)
-                slot = (h * 2 + way) * 4 + d - 1
-                lut[slot] = v.astype(BF)
-                cp = pltpu.make_async_remote_copy(
-                    src_ref=lut.at[slot], dst_ref=chain_in.at[h, way, d - 1],
-                    send_sem=ch_send.at[slot], recv_sem=ch_recv.at[h, way, d - 1],
-                    device_id=(dp, to), device_id_type=MESH,
-                )
-                cp.start()
-                links.append(cp)
+    def chain(d, h):
+        for way, (sign, to) in enumerate(((1, up_z), (-1, down_z))):
+            far = REACH[h][way]
+            if d > far:
+                continue
+            v = slab_sum(h, sign * d)
+            if d < far:
+                await_bytes(chain_in.at[h, way, d], ch_recv.at[h, way, d])
+                v = v + chain_in[h, way, d].astype(F32)
+            slot = (h * 2 + way) * 4 + d - 1
+            lut[slot] = v.astype(BF)
+            cp = pltpu.make_async_remote_copy(
+                src_ref=lut.at[slot], dst_ref=chain_in.at[h, way, d - 1],
+                send_sem=ch_send.at[slot], recv_sem=ch_recv.at[h, way, d - 1],
+                device_id=(dp, to), device_id_type=MESH,
+            )
+            cp.start()
+            links.append(cp)
 
     def part_in(b):
         return dot(stacked(0, b), xall[0, b]) + dot(stacked(1, b), xall[1, b])
 
-    chain(4)
-    ring1(3)
-    chain(3)
-    ring3(0)
-    ring2(3)
-    ring2(2)
-    chain(2)
-    ring3(1)
-    chain(1)
-    ring2(4)
-    ring3(3)
-    for h in range(2):
+    def tokens_grad(h):
         v = slab_sum(h, 0)
         for way in range(2):
             await_bytes(chain_in.at[h, way, 0], ch_recv.at[h, way, 0])
             v = v + chain_in[h, way, 0].astype(F32)
         dx_v[h * HALF:(h + 1) * HALF, :] = v.astype(BF)
-    store(dx_v, dx_o)
-    ring4(0)
-    ring4(1)
-
-    ring4(3)
+
+    for_sibling(0)
+    chain(4, 0)
+    chain(3, 0)
+    for_sibling(1)
+    chain(4, 1)
+    cross_first()
+    chain(2, 0)
+    relay(dm, rdm, m_send.at[3], m_recv.at[3], 7, 15, 1)
+    ring1(3)
+    ring2(2)
+    ring3(0)
+    chain(3, 1)
+    ring2(3)
+    outputs()
+    ring2(5)
+    chain(1, 0)
+    ring3(1)
+    chain(2, 1)
+
+    ring3(3)
     final = []
     for par in range(2):
         for cs in range(2):
@@ -568,12 +616,21 @@
             apart(*to, keep, away.start)
             final.append((to, away))
     ring3(2)
+    ring2(4)
+    tokens_grad(0)
+    chain(1, 1)
+    ring4(0)
+    ring3(5)
     ring3(4)
+    ring4(1)
+    tokens_grad(1)
+    store(dx_v, dx_o)
+    ring4(2)
+    ring4(5)
     await_bytes(wfin, wf_recv.at[0])
     for gu, (out, out_h) in enumerate(((rg_v, rg_o), (ru_v, ru_o))):
         out[...] = jnp.concatenate([wfin[j, gu * KW:(gu + 1) * KW, :] for j in range(4)], axis=0).T
         store(out, out_h.at[0])
-    ring4(2)
     ring4(4)
 
     for h in range(2):
@@ -582,13 +639,15 @@
     await_bytes(rdd.at[:, :, pl.ds(0, 480)], d_send.at[1])
     await_bytes(wp.at[0, pl.ds(0, 15)], w_send.at[0])
     await_bytes(wp.at[pl.ds(0, 3)], w_send.at[1])
-    await_bytes(rdm.at[:, :, pl.ds(0, 480)], m_send.at[2])
+    for h in range(2):
+        await_bytes(rdm.at[:, h, pl.ds(0, 480)], m_send.at[2 + h])
     for cp in crossing + links + downs:
         cp.wait_send()
     await_bytes(sums_in, s_send.at[0])
-    for group in started:
+    for group in started + [crossed]:
         for cp in group:
-            cp.wait_send()
+            if cp is not None:
+                cp.wait_send()
     for to, away in final:
         apart(*to, lambda: None, away.wait_send)
     for cp in stores:
@@ -637,11 +696,12 @@
         wide, wide, mids, mids, mids,
         V((3, 2, 128, MB), BF), V((3, 2, 128, MB), BF), V((3, 2, 128, MB), BF), V((3, 128, MB), BF),
         V((3, 128, MB), BF), V((3, 128, MB), BF), V((3, 2, 128, MB), BF), V((3, 2, 128, MB), BF), V((3, 128, MB), BF),
-        V((14, 256, DB), BF), V((14, 128, DB), BF), V((256, DB), F32), V((128, DB), F32), V((256, DB), BF), V((4, 64, DB), BF),
+        V((14, 128, DB), BF), V((14, 128, DB), BF), V((4, 2, 128, DB), BF), V((4, 2, 128, DB), BF),
+        V((128, DB), F32), V((256, DB), BF), V((4, 64, DB), BF),
         dma((9,)), dma((8,)), dma((2,)), dma((2, 8)), dma((2, 8)), dma((2,)), dma((2,)), dma((2,)), dma((2,)),
         dma((2,)), dma((2,)),
-        dma((3,)), dma((3,)), dma((25,)), dma((25,)),
-        dma((2,)), dma((2,)), dma((1,)), dma((2, 8)), dma((16,)), dma((2, 2, 4)), dma((4,)), dma((1,)),
+        dma((4,)), dma((4,)), dma((30,)), dma((30,)), dma((4,)), dma((4,)),
+        dma((4,)), dma((4,)), dma((1,)), dma((2, 8)), dma((16,)), dma((2, 2, 4)), dma((4,)), dma((1,)),
     ]
     results = pl.pallas_call(
         kernel,

time: 145 us -> 138 us (0.952)
  the two profiles are of different devices: /device:TPU:1 before, /device:TPU:83 now
where the time goes in v4:
time: 138 us
  Pallas kernels  137 us (99%)
    pallas_call x1, Pallas kernels, per_device(): pl.pallas_call(kernel, out_shape=out_shape, in_specs=[anyw] * 8, out_spec...  135 us

profile of v4, /device:TPU:83, one launch (start us, length us, event | category | flops | bytes accessed | tf_op | source)
XLA Modules:
  0.0 138.0 jit_solution(11633507834904548200)
XLA Ops:
  0.6 135.0 %shard_map.143 = (bf16[512,256]{1,0:T(8,128)(2,1)}, bf16[512,256]{1,0:T(8,128)(2,1)}, bf16[1,256,128]{2,1,0:T(8,128)(2,1)}, bf16[1,128,1024]{2,1,0:T(8,128)(2,1)...) custom-call(bf16[512,256]{1,0:T(8,128)(2,1)} %x_h.1, ...), custom_call_target="tpu_custom_call" | custom-call | flops 12000000000 | bytes 10000000 | tf_op jit(solution)/shard_map/pallas_call | solution.py:706
  135.7 2.2 %shard_map.144 = (bf16[512,256]{1,0:T(8,128)(2,1)}, bf16[512,256]{1,0:T(8,128)(2,1)}, bf16[1,256,128]{2,1,0:T(8,128)(2,1)}, bf16[1,128,1024]{2,1,0:T(8,128)(2,1)...) custom-call(bf16[512,256]{1,0:T(8,128)(2,1)} %get-tuple-element.16.r, ...), custom_call_target="tpu_custom_call" | custom-call | tf_op jit(solution)/shard_map/pallas_call | solution.py:717

commit v5 on v4

--- a/solution.py
+++ b/solution.py
@@ -493,12 +493,12 @@
             src = pl.ds(pl.multiple_of(yh * 512 + q * 256, 256), 256)
             back[yh, gu, h, q * 256:(q + 1) * 256, :] = dot(w[src, :], d[h]).astype(BF)
 
-    downs[0].wait_recv()
-    relay(dm, rdm, m_send.at[2], m_recv.at[2], 0, 15, 0)
     ring1(0)
     backward(0)
     mids_over(0, 0)
     mids_over(1, 0)
+    downs[0].wait_recv()
+    relay(dm, rdm, m_send.at[2], m_recv.at[2], 0, 15, 0)
     backward(1)
     mids_over(0, 1)
     mids_over(1, 1)

time: 138 us -> 136 us (0.986)
  the two profiles are of different devices: /device:TPU:83 before, /device:TPU:1 now
where the time goes in v5:
time: 136 us; the launch traced here: 135 us
  Pallas kernels  135 us (99%)
    pallas_call x1, Pallas kernels, per_device(): pl.pallas_call(kernel, out_shape=out_shape, in_specs=[anyw] * 8, out_spec...  132 us

profile of v5, /device:TPU:1, one launch (start us, length us, event | category | flops | bytes accessed | tf_op | source)
XLA Modules:
  0.0 135.4 jit_solution(13147734394919222344)
XLA Ops:
  0.6 132.4 %shard_map.143 = (bf16[512,256]{1,0:T(8,128)(2,1)}, bf16[512,256]{1,0:T(8,128)(2,1)}, bf16[1,256,128]{2,1,0:T(8,128)(2,1)}, bf16[1,128,1024]{2,1,0:T(8,128)(2,1)...) custom-call(bf16[512,256]{1,0:T(8,128)(2,1)} %x_h.1, ...), custom_call_target="tpu_custom_call" | custom-call | flops 12000000000 | bytes 10000000 | tf_op jit(solution)/shard_map/pallas_call | solution.py:706
  133.1 2.2 %shard_map.144 = (bf16[512,256]{1,0:T(8,128)(2,1)}, bf16[512,256]{1,0:T(8,128)(2,1)}, bf16[1,256,128]{2,1,0:T(8,128)(2,1)}, bf16[1,128,1024]{2,1,0:T(8,128)(2,1)...) custom-call(bf16[512,256]{1,0:T(8,128)(2,1)} %get-tuple-element.16.r, ...), custom_call_target="tpu_custom_call" | custom-call | tf_op jit(solution)/shard_map/pallas_call | solution.py:717

commit v6 on v5

--- a/solution.py
+++ b/solution.py
@@ -398,12 +398,9 @@
         if a == 3:
             crossed[0].wait_recv()
 
-        def put(half):
+        for half, (into, to) in enumerate(((ra, to_next), (rb, to_prev))):
             p2[half] = part(a, opp, half).astype(BF)
-
-        tiles(2, put)
-        started[a][0] = ship(p2.at[0], ra, 5 * a, to_next)
-        started[a][1] = ship(p2.at[1], rb, 5 * a + 1, to_prev)
+            started[a][half] = ship(p2.at[half], into, 5 * a + half, to)
 
     def ring2(a):
         _, pn, pp, _, ra, rb, rc, rdn, _ = places[a]

time: 136 us -> 136 us (level)
  no operation moved by 1% of the time
where the time goes in v6:
time: 136 us; the launch traced here: 135 us
  Pallas kernels  134 us (99%)
    pallas_call x1, Pallas kernels, per_device(): pl.pallas_call(kernel, out_shape=out_shape, in_specs=[anyw] * 8, out_spec...  132 us

profile of v6, /device:TPU:1, one launch (start us, length us, event | category | flops | bytes accessed | tf_op | source)
XLA Modules:
  0.0 135.0 jit_solution(12506993305301337724)
XLA Ops:
  0.6 132.0 %shard_map.143 = (bf16[512,256]{1,0:T(8,128)(2,1)}, bf16[512,256]{1,0:T(8,128)(2,1)}, bf16[1,256,128]{2,1,0:T(8,128)(2,1)}, bf16[1,128,1024]{2,1,0:T(8,128)(2,1)...) custom-call(bf16[512,256]{1,0:T(8,128)(2,1)} %x_h.1, ...), custom_call_target="tpu_custom_call" | custom-call | flops 12000000000 | bytes 10000000 | tf_op jit(solution)/shard_map/pallas_call | solution.py:703
  132.6 2.2 %shard_map.144 = (bf16[512,256]{1,0:T(8,128)(2,1)}, bf16[512,256]{1,0:T(8,128)(2,1)}, bf16[1,256,128]{2,1,0:T(8,128)(2,1)}, bf16[1,128,1024]{2,1,0:T(8,128)(2,1)...) custom-call(bf16[512,256]{1,0:T(8,128)(2,1)} %get-tuple-element.16.r, ...), custom_call_target="tpu_custom_call" | custom-call | tf_op jit(solution)/shard_map/pallas_call | solution.py:714
